TPU v7x, 32 devices: a whole 2x2x4 slice. The times are simulated.
32 devices in a mesh: rep: 4 (over y, x), shard: 8 (over z, core).
Axes of the slice: x: 2, y: 2, z: 4, core: 2. Of those that a mesh axis runs over, the one named last changes fastest.
Arguments:
- tokens: bfloat16 [32, 384, 768], P(('rep', 'shard')), may hold values from -6 to 6
- encoded: bfloat16 [32, 256, 768], P(('rep', 'shard')), may hold values from -6 to 6
- cotangent: bfloat16 [32, 384, 768], P(('rep', 'shard')), may hold values from -6 to 6
- buckets: int32 [384], replicated, may hold values from 0 to 31, as said below
- gains: bfloat16 [1, 3, 768], P(None, None, 'shard'), may hold values from 0.5 to 1.5
- self_query: bfloat16 [1, 768, 768], P(None, 'shard'), may hold values from -0.0546875 to 0.0546875
- self_kv: bfloat16 [1, 2, 768, 768], P(None, None, 'shard'), may hold values from -0.21875 to 0.21875
- self_out: bfloat16 [1, 768, 768], P(None, 'shard'), may hold values from -0.875 to 0.875
- cross_query: bfloat16 [1, 768, 768], P(None, 'shard'), may hold values from -0.0546875 to 0.0546875
- cross_kv: bfloat16 [1, 2, 768, 768], P(None, None, 'shard'), may hold values from -0.21875 to 0.21875
- cross_out: bfloat16 [1, 768, 768], P(None, 'shard'), may hold values from -0.875 to 0.875
- ffn_in: bfloat16 [1, 2, 768, 2048], P(None, None, 'shard'), may hold values from -0.21875 to 0.21875
- ffn_out: bfloat16 [1, 2048, 768], P(None, 'shard'), may hold values from -0.1875 to 0.1875
- bias_table: bfloat16 [32, 12], P('shard'), may hold values from -4 to 4
Outputs:
- layer_output: bfloat16 [32, 384, 768], P(('rep', 'shard'))
- grad_tokens: float32 [32, 384, 768], P(('rep', 'shard'))
- grad_encoded: float32 [32, 256, 768], P(('rep', 'shard'))
- grad_gains: float32 [1, 3, 768], P(None, None, 'shard')
- grad_self_query: float32 [1, 768, 768], P(None, 'shard')
- grad_self_kv: float32 [1, 2, 768, 768], P(None, None, 'shard')
- grad_self_out: float32 [1, 768, 768], P(None, 'shard')
- grad_cross_query: float32 [1, 768, 768], P(None, 'shard')
- grad_cross_kv: float32 [1, 2, 768, 768], P(None, None, 'shard')
- grad_cross_out: float32 [1, 768, 768], P(None, 'shard')
- grad_ffn_in: float32 [1, 2, 768, 2048], P(None, None, 'shard')
- grad_ffn_out: float32 [1, 2048, 768], P(None, 'shard')
- grad_bias_table: float32 [32, 12], P('shard')
Inputs may be any that keep to these rules, and one draw needn't show every extreme that they name: `buckets`: never falls as the distance grows, equals the distance below 16, and is 31 at the distance 384 - 1.
All inputs are finite; a program needn't handle non-finite values.
Results may differ from a plain program's by a relative error of at most 0.023.
The roundings to bfloat16 on the way count: a program that leaves them out, or rounds other values in their place, can miss the bound.
Values may be sent and summed in bfloat16 or wider, within the bound.
A program may use at most 192 MiB of HBM per device.

v0:
```python
from functools import partial

import jax
import jax.numpy as jnp
from jax import lax
from jax.sharding import PartitionSpec as P

HEADS = 12
HEAD = 64
NB = 32
LAYERS = 1


negative = -1e30
epsilon = 1e-06
highest = lax.Precision.HIGHEST
tanh_scale = 0.7978845608028654


def smooth_gate(value):
    return 0.5 * value * (1.0 + jnp.tanh(tanh_scale * (value + 0.044715 * value * value * value)))


def gated(gate, up):
    return smooth_gate(gate) * up


def root_norm(rows, gain):
    return rows * lax.rsqrt(jnp.mean(rows * rows, axis=-1, keepdims=True) + epsilon) * gain


def product(left, right):
    return jnp.dot(left, right, preferred_element_type=jnp.float32)


def inner_rows(left, right):
    return lax.dot_general(
        left, right, (((0,), (0,)), ((), ())), preferred_element_type=jnp.float32
    )


def outer_rows(left, right):
    return lax.dot_general(
        left, right, (((1,), (1,)), ((), ())), preferred_element_type=jnp.float32
    )


def split_heads(block):
    return block.reshape(block.shape[0], HEADS, HEAD)


def per_sequence(block, count):
    return block.reshape(count, -1, block.shape[-1])


def scores_of(query, keys, bias):
    return (
        jnp.einsum(
            "qhd,khd->hqk",
            split_heads(query),
            split_heads(keys),
            preferred_element_type=jnp.float32,
        )
        + bias
    )


def attend_forward(bias, items):
    query, keys, values = items
    scores = scores_of(query, keys, bias)
    top = jnp.max(scores, axis=-1, keepdims=True)
    log_total = top + jnp.log(jnp.sum(jnp.exp(scores - top), axis=-1, keepdims=True))
    probs = jnp.exp(scores - log_total).astype(jnp.bfloat16)
    mixed = jnp.einsum(
        "hqk,khd->qhd", probs, split_heads(values), preferred_element_type=jnp.float32
    )
    return (mixed.reshape(query.shape).astype(jnp.bfloat16), log_total)


def attend_backward(bias, items):
    query, keys, values, log_total, grad_mixed = items
    probs = jnp.exp(scores_of(query, keys, bias) - log_total)
    upstream = split_heads(grad_mixed)
    grad_values = jnp.einsum(
        "hqk,qhd->khd", probs.astype(jnp.bfloat16), upstream, preferred_element_type=jnp.float32
    )
    grad_probs = jnp.einsum(
        "qhd,khd->hqk", upstream, split_heads(values), preferred_element_type=jnp.float32
    )
    grad_scores = probs * (grad_probs - jnp.sum(probs * grad_probs, axis=-1, keepdims=True))
    rounded = grad_scores.astype(jnp.bfloat16)
    grad_query = jnp.einsum(
        "hqk,khd->qhd", rounded, split_heads(keys), preferred_element_type=jnp.float32
    )
    grad_keys = jnp.einsum(
        "hqk,qhd->khd", rounded, split_heads(query), preferred_element_type=jnp.float32
    )
    grads = (
        grad_query.reshape(query.shape).astype(jnp.bfloat16),
        grad_keys.reshape(keys.shape).astype(jnp.bfloat16),
        grad_values.reshape(values.shape).astype(jnp.bfloat16),
    )
    return (grads, grad_scores)


def offset_sums(grid):
    heads_count = grid.shape[0]
    length = grid.shape[-1]
    flipped = grid[..., ::-1]
    padded = jnp.concatenate([flipped, jnp.zeros_like(flipped)], axis=-1)
    flat = padded.reshape(heads_count, -1)[:, : length * (2 * length - 1)]
    skewed = flat.reshape(heads_count, length, 2 * length - 1)
    return jnp.sum(skewed, axis=1)[:, length - 1 :]


def cross_back(items):
    return attend_backward(0.0, items)[0]


def self_back(bias, items):
    grads, grad_scores = attend_backward(bias, items)
    return (grads, offset_sums(grad_scores))


def position_bias(table, onehot, length):
    per_offset = jnp.einsum("ob,bh->ho", onehot, table.astype(jnp.float32), precision=highest)
    distance = jnp.arange(length)[:, None] - jnp.arange(length)[None, :]
    return jnp.where(
        distance[None] >= 0, per_offset[:, jnp.clip(distance, 0, length - 1)], negative
    )


def layer_forward(residual, encoded, weights, bias):
    (
        gains,
        self_query,
        self_kv,
        self_out,
        cross_query,
        cross_kv,
        cross_out,
        ffn_in,
        ffn_out,
        table,
    ) = weights
    count = encoded.shape[0]
    width = residual.shape[1]
    enc_rows = encoded.reshape(-1, width)
    normed_self = root_norm(residual, gains[0].astype(jnp.float32)).astype(jnp.bfloat16)
    query = product(normed_self, self_query).astype(jnp.bfloat16)
    keys = product(normed_self, self_kv[0]).astype(jnp.bfloat16)
    values = product(normed_self, self_kv[1]).astype(jnp.bfloat16)
    mixed, log_self = lax.map(
        partial(attend_forward, bias),
        (per_sequence(query, count), per_sequence(keys, count), per_sequence(values, count)),
    )
    mixed = mixed.reshape(-1, width)
    after_self = residual + product(mixed, self_out)
    normed_cross = root_norm(after_self, gains[1].astype(jnp.float32)).astype(jnp.bfloat16)
    cross_q = product(normed_cross, cross_query).astype(jnp.bfloat16)
    cross_k = product(enc_rows, cross_kv[0]).astype(jnp.bfloat16)
    cross_v = product(enc_rows, cross_kv[1]).astype(jnp.bfloat16)
    cross_mixed, log_cross = lax.map(
        partial(attend_forward, 0.0),
        (per_sequence(cross_q, count), per_sequence(cross_k, count), per_sequence(cross_v, count)),
    )
    cross_mixed = cross_mixed.reshape(-1, width)
    after_cross = after_self + product(cross_mixed, cross_out)
    normed_ffn = root_norm(after_cross, gains[2].astype(jnp.float32)).astype(jnp.bfloat16)
    gate = product(normed_ffn, ffn_in[0])
    up = product(normed_ffn, ffn_in[1])
    hidden = gated(gate, up).astype(jnp.bfloat16)
    output = after_cross + product(hidden, ffn_out)
    kept = (
        residual,
        after_self,
        after_cross,
        normed_self,
        query,
        keys,
        values,
        mixed,
        log_self,
        normed_cross,
        cross_q,
        cross_k,
        cross_v,
        cross_mixed,
        log_cross,
        normed_ffn,
        gate,
        up,
        hidden,
    )
    return (output, kept)


def layer_backward(grad_rows, encoded, weights, bias, kept, onehot):
    (
        gains,
        self_query,
        self_kv,
        self_out,
        cross_query,
        cross_kv,
        cross_out,
        ffn_in,
        ffn_out,
        table,
    ) = weights
    (
        residual,
        after_self,
        after_cross,
        normed_self,
        query,
        keys,
        values,
        mixed,
        log_self,
        normed_cross,
        cross_q,
        cross_k,
        cross_v,
        cross_mixed,
        log_cross,
        normed_ffn,
        gate,
        up,
        hidden,
    ) = kept
    count = encoded.shape[0]
    width = grad_rows.shape[1]
    enc_rows = encoded.reshape(-1, width)
    branch = grad_rows.astype(jnp.bfloat16)
    grad_ffn_out = inner_rows(hidden, branch)
    unused, pull = jax.vjp(gated, gate, up)
    grad_gate, grad_up = pull(outer_rows(branch, ffn_out))
    grad_gate = grad_gate.astype(jnp.bfloat16)
    grad_up = grad_up.astype(jnp.bfloat16)
    grad_ffn_in = jnp.stack([inner_rows(normed_ffn, grad_gate), inner_rows(normed_ffn, grad_up)])
    grad_normed = outer_rows(grad_gate, ffn_in[0]) + outer_rows(grad_up, ffn_in[1])
    unused, pull = jax.vjp(root_norm, after_cross, gains[2].astype(jnp.float32))
    grad_back, gain_ffn = pull(grad_normed)
    grad_rows = grad_rows + grad_back
    branch = grad_rows.astype(jnp.bfloat16)
    grad_cross_out = inner_rows(cross_mixed, branch)
    grad_mixed = outer_rows(branch, cross_out).astype(jnp.bfloat16)
    grad_cq, grad_ck, grad_cv = lax.map(
        cross_back,
        (
            per_sequence(cross_q, count),
            per_sequence(cross_k, count),
            per_sequence(cross_v, count),
            log_cross,
            per_sequence(grad_mixed, count),
        ),
    )
    grad_cq = grad_cq.reshape(-1, width)
    grad_ck = grad_ck.reshape(-1, width)
    grad_cv = grad_cv.reshape(-1, width)
    grad_cross_query = inner_rows(normed_cross, grad_cq)
    grad_cross_kv = jnp.stack([inner_rows(enc_rows, grad_ck), inner_rows(enc_rows, grad_cv)])
    grad_states = outer_rows(grad_ck, cross_kv[0]) + outer_rows(grad_cv, cross_kv[1])
    unused, pull = jax.vjp(root_norm, after_self, gains[1].astype(jnp.float32))
    grad_back, gain_cross = pull(outer_rows(grad_cq, cross_query))
    grad_rows = grad_rows + grad_back
    branch = grad_rows.astype(jnp.bfloat16)
    grad_self_out = inner_rows(mixed, branch)
    grad_mixed = outer_rows(branch, self_out).astype(jnp.bfloat16)
    (grad_query, grad_keys, grad_values), offsets = lax.map(
        partial(self_back, bias),
        (
            per_sequence(query, count),
            per_sequence(keys, count),
            per_sequence(values, count),
            log_self,
            per_sequence(grad_mixed, count),
        ),
    )
    grad_query = grad_query.reshape(-1, width)
    grad_keys = grad_keys.reshape(-1, width)
    grad_values = grad_values.reshape(-1, width)
    grad_self_query = inner_rows(normed_self, grad_query)
    grad_self_kv = jnp.stack(
        [inner_rows(normed_self, grad_keys), inner_rows(normed_self, grad_values)]
    )
    grad_normed = (
        outer_rows(grad_query, self_query)
        + outer_rows(grad_keys, self_kv[0])
        + outer_rows(grad_values, self_kv[1])
    )
    unused, pull = jax.vjp(root_norm, residual, gains[0].astype(jnp.float32))
    grad_back, gain_self = pull(grad_normed)
    grad_rows = grad_rows + grad_back
    grad_table = jnp.einsum("ho,ob->bh", jnp.sum(offsets, axis=0), onehot, precision=highest)
    grads = (
        jnp.stack([gain_self, gain_cross, gain_ffn]),
        grad_self_query,
        grad_self_kv,
        grad_self_out,
        grad_cross_query,
        grad_cross_kv,
        grad_cross_out,
        grad_ffn_in,
        grad_ffn_out,
        grad_table,
    )
    return (grad_rows, grad_states, grads)


def shards(
    tokens,
    encoded,
    cotangent,
    buckets,
    gains,
    self_query,
    self_kv,
    self_out,
    cross_query,
    cross_kv,
    cross_out,
    ffn_in,
    ffn_out,
    bias_table,
):
    count, length, width = tokens.shape
    onehot = (buckets[:, None] == jnp.arange(NB)[None, :]).astype(jnp.float32)
    rows = tokens.reshape(-1, width).astype(jnp.float32)
    index = 0
    weights = (
        lax.all_gather(gains[index], "shard", axis=1, tiled=True),
        lax.all_gather(self_query[index], "shard", axis=0, tiled=True),
        lax.all_gather(self_kv[index], "shard", axis=1, tiled=True),
        lax.all_gather(self_out[index], "shard", axis=0, tiled=True),
        lax.all_gather(cross_query[index], "shard", axis=0, tiled=True),
        lax.all_gather(cross_kv[index], "shard", axis=1, tiled=True),
        lax.all_gather(cross_out[index], "shard", axis=0, tiled=True),
        lax.all_gather(ffn_in[index], "shard", axis=1, tiled=True),
        lax.all_gather(ffn_out[index], "shard", axis=0, tiled=True),
        lax.all_gather(bias_table, "shard", axis=0, tiled=True),
    )
    rows, kept = layer_forward(rows, encoded, weights, position_bias(weights[9], onehot, length))
    saved = [(None, kept)]
    grad_rows = cotangent.reshape(-1, width).astype(jnp.float32)
    grad_states = jnp.zeros((encoded.shape[0] * encoded.shape[1], width), jnp.float32)
    shares = []
    for index in reversed(range(LAYERS)):
        weights = (
            lax.all_gather(gains[index], "shard", axis=1, tiled=True),
            lax.all_gather(self_query[index], "shard", axis=0, tiled=True),
            lax.all_gather(self_kv[index], "shard", axis=1, tiled=True),
            lax.all_gather(self_out[index], "shard", axis=0, tiled=True),
            lax.all_gather(cross_query[index], "shard", axis=0, tiled=True),
            lax.all_gather(cross_kv[index], "shard", axis=1, tiled=True),
            lax.all_gather(cross_out[index], "shard", axis=0, tiled=True),
            lax.all_gather(ffn_in[index], "shard", axis=1, tiled=True),
            lax.all_gather(ffn_out[index], "shard", axis=0, tiled=True),
            lax.all_gather(bias_table, "shard", axis=0, tiled=True),
        )
        grad_rows, grad_part, grads = layer_backward(
            grad_rows,
            encoded,
            weights,
            position_bias(weights[9], onehot, length),
            saved[index][1],
            onehot,
        )
        grad_states = grad_part
        share = (
            lax.psum_scatter(grads[0], "shard", scatter_dimension=1, tiled=True),
            lax.psum_scatter(grads[1], "shard", scatter_dimension=0, tiled=True),
            lax.psum_scatter(grads[2], "shard", scatter_dimension=1, tiled=True),
            lax.psum_scatter(grads[3], "shard", scatter_dimension=0, tiled=True),
            lax.psum_scatter(grads[4], "shard", scatter_dimension=0, tiled=True),
            lax.psum_scatter(grads[5], "shard", scatter_dimension=1, tiled=True),
            lax.psum_scatter(grads[6], "shard", scatter_dimension=0, tiled=True),
            lax.psum_scatter(grads[7], "shard", scatter_dimension=1, tiled=True),
            lax.psum_scatter(grads[8], "shard", scatter_dimension=0, tiled=True),
            lax.psum_scatter(grads[9], "shard", scatter_dimension=0, tiled=True),
        )
        share = lax.psum(
            (
                share[0],
                share[1],
                share[2],
                share[3],
                share[4],
                share[5],
                share[6],
                share[7],
                share[8],
                share[9],
            ),
            "rep",
        )
        shares.insert(0, share)
    stacked = tuple((jnp.stack([share[item] for share in shares]) for item in range(9)))
    table_grad = shares[0][9]
    final = stacked + (table_grad,)
    return (
        rows.astype(jnp.bfloat16).reshape(tokens.shape),
        grad_rows.reshape(tokens.shape),
        grad_states.reshape(encoded.shape),
        final[0],
        final[1],
        final[2],
        final[3],
        final[4],
        final[5],
        final[6],
        final[7],
        final[8],
        final[9],
    )


def solution(mesh):
    return jax.shard_map(
        shards,
        mesh=mesh,
        in_specs=(
            P(("rep", "shard"), None, None),
            P(("rep", "shard"), None, None),
            P(("rep", "shard"), None, None),
            P(),
            P(None, None, "shard"),
            P(None, "shard", None),
            P(None, None, "shard", None),
            P(None, "shard", None),
            P(None, "shard", None),
            P(None, None, "shard", None),
            P(None, "shard", None),
            P(None, None, "shard", None),
            P(None, "shard", None),
            P("shard", None),
        ),
        out_specs=(
            P(("rep", "shard"), None, None),
            P(("rep", "shard"), None, None),
            P(("rep", "shard"), None, None),
            P(None, None, "shard"),
            P(None, "shard", None),
            P(None, None, "shard", None),
            P(None, "shard", None),
            P(None, "shard", None),
            P(None, None, "shard", None),
            P(None, "shard", None),
            P(None, None, "shard", None),
            P(None, "shard", None),
            P("shard", None),
        ),
        check_vma=False,
    )
```

profile of v0, /device:TPU:0, one launch (start us, length us, event | category | flops | bytes accessed | tf_op | source)
XLA Modules:
  0.0 1390.1 jit_solution(2961534045005626104)
XLA Ops:
  13.0 17.1 %all-gather = bf16[1,3,768]{1,0,2:T(2,128)(2,1)S(1)} all-gather(bf16[1,3,96]{1,0,2:T(2,128)(2,1)S(1)} %copy.98), channel_id=2, replica_groups=mesh['rep'=4,'shard'=8] {'shard'}, dimensions={2}, use_global_device_ids=true | all-gather | bytes 5184 | tf_op jit(solution)/shard_map/all_gather | solution.py:333
  30.1 7.8 fusion.76
  38.2 11.8 all-gather.9
  50.5 487.4 %gather_fusion = f32[147456,12]{1,0:T(8,128)} fusion(f32[12,384]{0,1:T(8,128)S(1)} %copy.102, s32[147456]{0:T(1024)S(1)} %broadcast_clamp_fusion), kind=kCustom, calls=%fused_computation | custom fusion | bytes 14745600 | tf_op jit(solution)/shard_map/gather | solution.py:129
  537.9 42.7 %copy.104 = f32[384,384,12]{0,1,2:T(8,128)} copy(f32[384,384,12]{2,1,0:T(8,128)} %bitcast.11) | data formatting | bytes 14155776 | tf_op jit(solution)/shard_map/gather | solution.py:129
  585.4 3.0 convolution_convert_fusion.7
  589.8 2.7 convolution_convert_fusion.13
  593.6 4.4 fusion.105
  605.2 2.8 convolution_convert_fusion.5
  609.4 2.7 convolution_convert_fusion.12
  623.0 5.3 fusion.13
  628.3 3.4 fusion.15
  631.8 8.0 multiply_convert_fusion.1
  639.7 4.4 fusion.12
  644.2 3.6 multiply_reduce_fusion.2
  652.2 3.5 multiply_reduce_fusion.1
  663.1 2.4 pad_maximum_fusion.2
  665.5 8.2 copy.118
  679.6 7.8 multiply_reduce_fusion
  687.5 7.2 subtract_multiply_fusion
  694.6 3.8 fusion.34
  701.6 3.2 fusion.83
  705.9 2.3 fusion.98
  712.9 4.5 convolution_convert_fusion
  719.2 4.4 fusion.37
  725.4 2.5 pad_maximum_fusion.1
  729.4 4.5 fusion.71
  734.0 3.6 convolution_bitcast_fusion
  737.6 4.5 convolution_bitcast_fusion.1
  742.1 9.0 pad_maximum_fusion
  758.9 19.6 %all-reduce.8.cloned.1.call-done = f32[2,768,768]{2,0,1:T(2,128)} async-done(((f32[2,768,768]{2,0,1:T(2,128)}), f32[2,768,768]{2,0,1:T(2,128)}) %all-reduce.8.cloned.1.call-update) | async-done | bytes 4718608
  780.4 36.6 %reduce-scatter.11.cloned.1.call-done = f32[96,768]{1,0:T(8,128)} async-done(((f32[768,768]{1,0:T(8,128)}), f32[96,768]{1,0:T(8,128)}) %reduce-scatter.11.cloned.1.call-update) | async-done | bytes 294928 | tf_op jit(solution)/shard_map/reduce_scatter | solution.py:373
  817.0 37.8 %reduce-scatter.15.cloned.1.call-done = f32[96,768]{1,0:T(8,128)} async-done(((f32[768,768]{1,0:T(8,128)}), f32[96,768]{1,0:T(8,128)}) %reduce-scatter.15.cloned.1.call-update) | async-done | bytes 294928 | tf_op jit(solution)/shard_map/reduce_scatter | solution.py:375
  854.9 37.7 %reduce-scatter.17.cloned.1.call-done = f32[96,768]{1,0:T(8,128)} async-done(((f32[768,768]{1,0:T(8,128)}), f32[96,768]{1,0:T(8,128)}) %reduce-scatter.17.cloned.1.call-update) | async-done | bytes 294928 | tf_op jit(solution)/shard_map/reduce_scatter | solution.py:376
  892.6 37.8 %reduce-scatter.19.cloned.1.call-done = f32[96,768]{1,0:T(8,128)} async-done(((f32[768,768]{1,0:T(8,128)}), f32[96,768]{1,0:T(8,128)}) %reduce-scatter.19.cloned.1.call-update) | async-done | bytes 294928 | tf_op jit(solution)/shard_map/reduce_scatter | solution.py:378
  930.4 56.4 %reduce-scatter.13.cloned.1.call-done = f32[2,96,768]{2,1,0:T(8,128)} async-done(((f32[2,768,768]{2,1,0:T(8,128)}), f32[2,96,768]{2,1,0:T(8,128)}) %reduce-scatter.13.cloned.1.call-update) | async-done | bytes 589840 | tf_op jit(solution)/shard_map/reduce_scatter | solution.py:374
  986.8 70.3 %reduce-scatter.23.cloned.1.call-done = f32[256,768]{1,0:T(8,128)} async-done(((f32[2048,768]{1,0:T(8,128)}), f32[256,768]{1,0:T(8,128)}) %reduce-scatter.23.cloned.1.call-update) | async-done | bytes 786448 | tf_op jit(solution)/shard_map/reduce_scatter | solution.py:380
  1057.1 129.8 %reduce-scatter.21.cloned.1.call-done = f32[2,96,2048]{2,1,0:T(8,128)} async-done(((f32[2,768,2048]{2,1,0:T(8,128)}), f32[2,96,2048]{2,1,0:T(8,128)}) %reduce-scatter.21.cloned.1.call-update) | async-done | bytes 1572880 | tf_op jit(solution)/shard_map/reduce_scatter | solution.py:379
  1187.6 54.4 %rev.4 = f32[12,384,384]{1,2,0:T(8,128)} reverse(f32[12,384,384]{1,2,0:T(8,128)} %subtract_multiply_fusion), dimensions={2} | reverse | bytes 14155776 | tf_op jit(solution)/shard_map/while/body/eval_jaxpr/rev | solution.py:109
  1242.0 8.2 copy.134
  1250.2 4.5 concatenate.4.clone
  1256.7 25.4 %copy.135 = f32[2,8,384,768]{3,1,2,0:T(8,128)S(1)} copy(f32[2,8,384,768]{3,2,1,0:T(8,128)S(1)} %bitcast.252) | data formatting | bytes 37748736
  1282.1 7.4 slice.75
  1289.5 30.8 %reshape.404 = f32[12,384,767]{2,1,0:T(8,128)} reshape(f32[12,294528]{1,0:T(8,128)} %slice.75) | data formatting | bytes 28274688 | tf_op jit(solution)/shard_map/while/body/eval_jaxpr/reshape | solution.py:112
  1320.3 6.3 reduce_sum.159
  1327.0 25.9 %all-reduce.2 = f32[32,12]{1,0:T(8,128)S(1)} all-reduce(f32[32,12]{1,0:T(8,128)S(1)} %fusion.90), channel_id=20, replica_groups=mesh['rep'=4,'shard'=8] {'shard'}, use_global_device_ids=true, to_apply=%region_34.35.clone | all-reduce | flops 384 | bytes 3072
  1357.8 4.1 fusion.41
  1362.8 10.4 all-reduce.3
  (265 shorter events, 91.4 us)
Async XLA Ops:
  7.2 582.6 %copy-start = (bf16[1,256,768]{2,1,0:T(8,128)(2,1)S(1)}, bf16[1,256,768]{2,1,0:T(8,128)(2,1)}, u32[]{:S(2)}) copy-start(bf16[1,256,768]{2,1,0:T(8,128)(2,1)} %param.15) | copy-start | bytes 1179652
  7.2 5.7 copy-start.61
  7.2 573.4 %all-gather.21.cloned.1.call-start = ((), (), s32[]{:S(2)}) async-start(), calls=%async_computation.16 | async-start | bytes 1327104 | tf_op jit(solution)/shard_map/all_gather | solution.py:334
  7.9 575.0 %all-gather.19.cloned.1.call-start = ((), (), s32[]{:S(2)}) async-start(), calls=%async_computation.15 | async-start | bytes 2654208 | tf_op jit(solution)/shard_map/all_gather | solution.py:335
  8.7 581.1 %all-gather.25.cloned.1.call-start = ((), (), s32[]{:S(2)}) async-start(), calls=%async_computation.18 | async-start | bytes 2654208 | tf_op jit(solution)/shard_map/all_gather | solution.py:338
  9.4 593.5 %all-gather.23.cloned.1.call-start = ((), (), s32[]{:S(2)}) async-start(), calls=%async_computation.17 | async-start | bytes 1327104 | tf_op jit(solution)/shard_map/all_gather | solution.py:336
  10.0 595.2 %all-gather.27.cloned.1.call-start = ((), (), s32[]{:S(2)}) async-start(), calls=%async_computation.19 | async-start | bytes 1327104 | tf_op jit(solution)/shard_map/all_gather | solution.py:337
  10.6 609.1 %all-gather.29.cloned.1.call-start = ((), (), s32[]{:S(2)}) async-start(), calls=%async_computation.20 | async-start | bytes 1327104 | tf_op jit(solution)/shard_map/all_gather | solution.py:339
  11.2 611.9 %all-gather.31.cloned.1.call-start = ((), (), s32[]{:S(2)}) async-start(), calls=%async_computation.21 | async-start | bytes 7077888 | tf_op jit(solution)/shard_map/all_gather | solution.py:340
  11.9 26.1 %copy-start.8 = (bf16[1,384,768]{2,1,0:T(8,128)(2,1)S(1)}, bf16[1,384,768]{2,1,0:T(8,128)(2,1)}, u32[]{:S(2)}) copy-start(bf16[1,384,768]{2,1,0:T(8,128)(2,1)} %param.14) | copy-start | bytes 1769476
  11.9 619.8 %all-gather.33.cloned.1.call-start = ((), (), s32[]{:S(2)}) async-start(), calls=%async_computation.22 | async-start | bytes 3538944 | tf_op jit(solution)/shard_map/all_gather | solution.py:341
  12.7 25.5 %copy-start.62 = (bf16[4,12]{1,0:T(4,128)(2,1)S(1)}, bf16[4,12]{1,0:T(4,128)(2,1)}, u32[]{:S(2)}) copy-start(bf16[4,12]{1,0:T(4,128)(2,1)} %param.27) | copy-start | bytes 292
  12.7 37.3 %copy-start.64 = (s32[384]{0:T(512)S(1)}, s32[384]{0:T(512)}, u32[]{:S(2)}) copy-start(s32[384]{0:T(512)} %param.17) | copy-start | bytes 4612
  12.7 765.8 %all-reduce.8.cloned.1.call-start = ((), (), s32[]{:S(2)}) async-start(), calls=%async_computation.24 | async-start | bytes 9437184
  38.2 11.8 copy-start.59
  582.9 10.8 copy-start.15
  585.4 13.7 copy-start.19
  589.7 3.9 copy-start.17
  593.6 22.9 %copy-start.32 = (bf16[256,768]{0,1:T(8,128)(2,1)}, bf16[256,768]{0,1:T(8,128)(2,1)S(1)}, u32[]{:S(2)}) copy-start(bf16[256,768]{0,1:T(8,128)(2,1)S(1)} %copy.106) | copy-start | bytes 1179652
  609.4 4.6 copy-start.24
  621.8 26.0 %copy-start.11 = (f32[384,768]{1,0:T(8,128)}, f32[384,768]{1,0:T(8,128)S(1)}, u32[]{:S(2)}) copy-start(f32[384,768]{1,0:T(8,128)S(1)} %get-tuple-element.193) | copy-start | bytes 3538948
  623.0 5.3 copy-start.21
  623.0 5.3 copy-start.63
  639.7 4.5 copy-start.46
  639.7 4.5 copy-start.48
  658.8 3.7 copy-start.34
  673.7 143.3 %reduce-scatter.11.cloned.1.call-start = ((), (), s32[]{:S(2)}) async-start(), calls=%async_computation.8 | async-start | bytes 2654208 | tf_op jit(solution)/shard_map/reduce_scatter | solution.py:373
  676.0 25.6 %copy-start.4 = (f32[384,768]{1,0:T(8,128)}, f32[384,768]{1,0:T(8,128)S(1)}, u32[]{:S(2)}) copy-start(f32[384,768]{1,0:T(8,128)S(1)} %fusion.51) | copy-start | bytes 3538948
  679.6 7.8 slice-start
  679.6 7.8 slice-start.1
  687.5 7.2 copy-start.18
  701.5 153.4 %reduce-scatter.15.cloned.1.call-start = ((), (), s32[]{:S(2)}) async-start(), calls=%async_computation.10 | async-start | bytes 2654208 | tf_op jit(solution)/shard_map/reduce_scatter | solution.py:375
  704.8 187.8 %reduce-scatter.17.cloned.1.call-start = ((), (), s32[]{:S(2)}) async-start(), calls=%async_computation.11 | async-start | bytes 2654208 | tf_op jit(solution)/shard_map/reduce_scatter | solution.py:376
  708.2 222.2 %reduce-scatter.19.cloned.1.call-start = ((), (), s32[]{:S(2)}) async-start(), calls=%async_computation.12 | async-start | bytes 2654208 | tf_op jit(solution)/shard_map/reduce_scatter | solution.py:378
  711.8 275.0 %reduce-scatter.13.cloned.1.call-start = ((), (), s32[]{:S(2)}) async-start(), calls=%async_computation.9 | async-start | bytes 5308416 | tf_op jit(solution)/shard_map/reduce_scatter | solution.py:374
  727.9 329.2 %reduce-scatter.23.cloned.1.call-start = ((), (), s32[]{:S(2)}) async-start(), calls=%async_computation.14 | async-start | bytes 7077888 | tf_op jit(solution)/shard_map/reduce_scatter | solution.py:380
  733.9 453.0 %reduce-scatter.21.cloned.1.call-start = ((), (), s32[]{:S(2)}) async-start(), calls=%async_computation.13 | async-start | bytes 14155776 | tf_op jit(solution)/shard_map/reduce_scatter | solution.py:379
  751.2 610.8 %reduce-scatter.25.cloned.1.call-start = ((), (), s32[]{:S(2)}) async-start(), calls=%async_computation.23 | async-start | bytes 442368
  758.8 614.9 %all-reduce.10.cloned.1.call-start = ((), (), s32[]{:S(2)}) async-start(), calls=%async_computation.25 | async-start | bytes 9437184 | tf_op jit(solution)/shard_map/psum | solution.py:383
  1320.3 6.4 copy-start.65
  1320.3 32.7 %copy-start.60 = (f32[384]{0:T(512)S(1)}, f32[384]{0:T(512)}, u32[]{:S(2)}) copy-start(f32[384]{0:T(512)} %copy-done.59) | copy-start | bytes 4612
  1320.3 32.7 %copy-start.35 = (bf16[12,64,256]{2,1,0:T(8,128)(2,1)S(1)}, bf16[12,64,256]{2,1,0:T(8,128)(2,1)}, u32[]{:S(2)}) copy-start(bf16[12,64,256]{2,1,0:T(8,128)(2,1)} %copy-done.34) | copy-start | bytes 1179652
  1320.3 32.7 %copy-start.43 = (bf16[1,2,768,768]{3,2,1,0:T(8,128)(2,1)S(1)}, bf16[1,2,768,768]{3,2,1,0:T(8,128)(2,1)}, u32[]{:S(2)}) copy-start(bf16[1,2,768,768]{3,2,1,0:T(8,128)(2,1)} %all-gather.25.cloned.1.call-done) | copy-start | bytes 7077892
  1326.7 26.8 %copy-start.37 = (bf16[12,64,256]{2,1,0:T(8,128)(2,1)S(1)}, bf16[12,64,256]{2,1,0:T(8,128)(2,1)}, u32[]{:S(2)}) copy-start(bf16[12,64,256]{2,1,0:T(8,128)(2,1)} %copy-done.36) | copy-start | bytes 1179652
  1373.8 3.8 copy-start.54
  1373.8 4.6 copy-start.58
  1373.8 5.3 copy-start.57
  1375.8 4.0 copy-start.56
  (41 other events, 76.2 us)
Sparse Core Ops, SparseCore 0:
  9.7 27.0 all-gather.20
  38.4 31.2 all-gather.18
  71.3 30.7 all-gather.24
  103.6 21.7 all-gather.22
  126.9 22.4 all-gather.26
  150.8 22.4 all-gather.28
  174.9 64.4 all-gather.30
  241.0 36.9 all-gather.32
  673.8 104.6 all-reduce.7
  780.7 36.3 reduce-scatter.10
  819.4 35.4 reduce-scatter.14
  857.0 35.4 reduce-scatter.16
  894.9 35.4 reduce-scatter.18
  932.6 54.1 reduce-scatter.12
  988.9 68.1 reduce-scatter.22
  1059.3 127.5 reduce-scatter.20
  1189.6 28.9 reduce-scatter.24
  1224.2 113.2 all-reduce.9
where the time goes:
time: 1400 us; the launch traced here: 1390 us
  local copies, waits for them, and re-layouts  712 us (51%)
  waiting for transfers between devices  431 us (31%)
  matrix products  120 us (9%)
  blocking collectives  65.2 us (5%)
  other arithmetic  43.3 us (3%)
  between operations  16.8 us (1%)
    gather x2, local copies, waits for them, and re-layouts, position_bias(): per_offset[:, jnp.clip(distance, 0, length - 1)]  530 us
    reduce_scatter x1, waiting for transfers between devices, shards(): lax.psum_scatter(grads[7], 'shard', scatter_dimension=1, tiled=True)  130 us
    reduce_scatter x1, waiting for transfers between devices, shards(): lax.psum_scatter(grads[8], 'shard', scatter_dimension=0, tiled=True)  70.3 us
    unnamed x159, local copies, waits for them, and re-layouts  64.2 us
    reduce_scatter x1, waiting for transfers between devices, shards(): lax.psum_scatter(grads[2], 'shard', scatter_dimension=1, tiled=True)  56.4 us
    rev x1, local copies, waits for them, and re-layouts, offset_sums(): flipped = grid[..., ::-1]  54.4 us
    reduce_scatter x1, waiting for transfers between devices, shards(): lax.psum_scatter(grads[3], 'shard', scatter_dimension=0, tiled=True)  37.8 us
    reduce_scatter x1, waiting for transfers between devices, shards(): lax.psum_scatter(grads[6], 'shard', scatter_dimension=0, tiled=True)  37.8 us
  transfers between devices with their start and end apart: 18, of which 8 were waited for; matrix products, arithmetic and copies ran while one was open for 58% of the time, Pallas kernels for 0%

commit v1 on v0

v1 whole, which is shorter than its diff:
```python
from functools import partial

import jax
import jax.numpy as jnp
from jax import lax
from jax.experimental import pallas as pl
from jax.experimental.pallas import tpu as pltpu
from jax.sharding import PartitionSpec as P

HEADS = 12
HEAD = 64
NB = 32
LAYERS = 1


negative = -1e30
epsilon = 1e-06
highest = lax.Precision.HIGHEST
tanh_scale = 0.7978845608028654


def smooth_gate(value):
    return 0.5 * value * (1.0 + jnp.tanh(tanh_scale * (value + 0.044715 * value * value * value)))


def gated(gate, up):
    return smooth_gate(gate) * up


def root_norm(rows, gain):
    return rows * lax.rsqrt(jnp.mean(rows * rows, axis=-1, keepdims=True) + epsilon) * gain


def product(left, right):
    return jnp.dot(left, right, preferred_element_type=jnp.float32)


def inner_rows(left, right):
    return lax.dot_general(
        left, right, (((0,), (0,)), ((), ())), preferred_element_type=jnp.float32
    )


def outer_rows(left, right):
    return lax.dot_general(
        left, right, (((1,), (1,)), ((), ())), preferred_element_type=jnp.float32
    )


STRIP = 128
PAIR = 2 * HEAD


def bias_of(line, length):
    extent = line.shape[-1]
    base = jnp.broadcast_to(line, (STRIP, extent))
    base = pltpu.roll(base, 0, 1, stride=1, stride_axis=0)
    strips = [base[:, :length]]
    for strip in range(1, length // STRIP):
        turn = strip * STRIP
        strips.append(
            jnp.concatenate([base[:, extent - turn :], base[:, : length - turn]], axis=1)
        )
    return jnp.concatenate(strips, axis=0)


def distance_sums(grid):
    length = grid.shape[-1]
    extent = 2 * length
    total = None
    for strip in range(length // STRIP):
        turn = strip * STRIP
        part = grid[turn : turn + STRIP, :]
        pieces = [jnp.zeros((STRIP, length - turn), jnp.float32), part]
        if turn:
            pieces.append(jnp.zeros((STRIP, turn), jnp.float32))
        part = jnp.concatenate(pieces, axis=1)
        total = part if total is None else total + part
    step = STRIP // 2
    while step >= 8:
        total = total[:step] + pltpu.roll(total[step:], extent - step, 1)
        step //= 2
    result = total[0:1]
    for row in range(1, 8):
        result = result + pltpu.roll(total, extent - row, 1)[row : row + 1]
    return result


def probabilities(query, keys, bias):
    scores = outer_rows(query, keys)
    if bias is not None:
        scores = scores + bias
    top = jnp.max(scores, axis=-1, keepdims=True)
    log_total = top + jnp.log(jnp.sum(jnp.exp(scores - top), axis=-1, keepdims=True))
    return jnp.exp(scores - log_total)


def forward_kernel(biased, query_ref, keys_ref, values_ref, *refs):
    for half in range(2):
        lanes = slice(half * HEAD, (half + 1) * HEAD)
        bias = bias_of(refs[0][half], query_ref.shape[0]) if biased else None
        probs = probabilities(query_ref[:, lanes], keys_ref[:, lanes], bias)
        mixed = product(probs.astype(jnp.bfloat16), values_ref[:, lanes])
        refs[-1][:, lanes] = mixed.astype(jnp.bfloat16)


def backward_kernel(biased, query_ref, keys_ref, values_ref, upstream_ref, *refs):
    outs = refs[1:] if biased else refs
    for half in range(2):
        lanes = slice(half * HEAD, (half + 1) * HEAD)
        query, keys = query_ref[:, lanes], keys_ref[:, lanes]
        values, upstream = values_ref[:, lanes], upstream_ref[:, lanes]
        bias = bias_of(refs[0][half], query.shape[0]) if biased else None
        probs = probabilities(query, keys, bias)
        outs[2][:, lanes] = inner_rows(probs.astype(jnp.bfloat16), upstream).astype(jnp.bfloat16)
        grad_probs = outer_rows(upstream, values)
        grad_scores = probs * (
            grad_probs - jnp.sum(probs * grad_probs, axis=-1, keepdims=True)
        )
        rounded = grad_scores.astype(jnp.bfloat16)
        outs[0][:, lanes] = product(rounded, keys).astype(jnp.bfloat16)
        outs[1][:, lanes] = inner_rows(rounded, query).astype(jnp.bfloat16)
        if biased:
            outs[3][0, half] = distance_sums(grad_scores)


def attention(kernel, operands, count, line=None):
    backward = len(operands) == 4
    rows = [item.shape[0] // count for item in operands]
    specs = [pl.BlockSpec((extent, PAIR), lambda s, h: (s, h)) for extent in rows]
    width = operands[0].shape[1]
    outs = [operands[i] for i in ((0, 1, 2) if backward else (0,))]
    out_shape = [jax.ShapeDtypeStruct(item.shape, jnp.bfloat16) for item in outs]
    out_specs = [
        pl.BlockSpec((item.shape[0] // count, PAIR), lambda s, h: (s, h)) for item in outs
    ]
    if line is not None:
        extent = line.shape[-1]
        operands = operands + (line,)
        specs.append(pl.BlockSpec((2, 1, extent), lambda s, h: (h, 0, 0)))
        if backward:
            out_shape.append(jax.ShapeDtypeStruct((count, HEADS, 1, extent), jnp.float32))
            out_specs.append(pl.BlockSpec((1, 2, 1, extent), lambda s, h: (s, h, 0, 0)))
    pairs = rows[0] * rows[1] * count
    return pl.pallas_call(
        partial(kernel, line is not None),
        grid=(count, width // PAIR),
        in_specs=specs,
        out_specs=out_specs,
        out_shape=out_shape,
        compiler_params=pltpu.CompilerParams(vmem_limit_bytes=32 * 1024 * 1024),
        cost_estimate=pl.CostEstimate(
            flops=2 * pairs * width * (5 if backward else 2),
            bytes_accessed=2 * width * sum(rows) * count * 2,
            transcendentals=2 * pairs * HEADS,
        ),
    )(*operands)


def bias_lines(table, buckets):
    length = buckets.shape[0]
    place = jnp.arange(2 * length)
    turned = jnp.concatenate(
        [buckets[:1], jnp.zeros((length,), buckets.dtype), buckets[:0:-1]]
    )
    onehot = (turned[:, None] == jnp.arange(NB)[None, :]).astype(jnp.float32)
    lines = jnp.einsum("ob,bh->ho", onehot, table.astype(jnp.float32), precision=highest)
    allowed = (place == 0) | (place > length)
    return jnp.where(allowed[None], lines, negative)[:, None, :]


def table_gradient(sums, buckets):
    length = buckets.shape[0]
    onehot = (buckets[::-1, None] == jnp.arange(NB)[None, :]).astype(jnp.float32)
    return jnp.einsum("ho,ob->bh", sums[:, 1 : length + 1], onehot, precision=highest)


def layer_forward(residual, encoded, weights, line):
    (
        gains,
        self_query,
        self_kv,
        self_out,
        cross_query,
        cross_kv,
        cross_out,
        ffn_in,
        ffn_out,
        table,
    ) = weights
    count = encoded.shape[0]
    width = residual.shape[1]
    enc_rows = encoded.reshape(-1, width)
    normed_self = root_norm(residual, gains[0].astype(jnp.float32)).astype(jnp.bfloat16)
    query = product(normed_self, self_query).astype(jnp.bfloat16)
    keys = product(normed_self, self_kv[0]).astype(jnp.bfloat16)
    values = product(normed_self, self_kv[1]).astype(jnp.bfloat16)
    (mixed,) = attention(forward_kernel, (query, keys, values), count, line)
    after_self = residual + product(mixed, self_out)
    normed_cross = root_norm(after_self, gains[1].astype(jnp.float32)).astype(jnp.bfloat16)
    cross_q = product(normed_cross, cross_query).astype(jnp.bfloat16)
    cross_k = product(enc_rows, cross_kv[0]).astype(jnp.bfloat16)
    cross_v = product(enc_rows, cross_kv[1]).astype(jnp.bfloat16)
    (cross_mixed,) = attention(forward_kernel, (cross_q, cross_k, cross_v), count)
    after_cross = after_self + product(cross_mixed, cross_out)
    normed_ffn = root_norm(after_cross, gains[2].astype(jnp.float32)).astype(jnp.bfloat16)
    gate = product(normed_ffn, ffn_in[0])
    up = product(normed_ffn, ffn_in[1])
    hidden = gated(gate, up).astype(jnp.bfloat16)
    output = after_cross + product(hidden, ffn_out)
    kept = (
        residual,
        after_self,
        after_cross,
        normed_self,
        query,
        keys,
        values,
        mixed,
        normed_cross,
        cross_q,
        cross_k,
        cross_v,
        cross_mixed,
        normed_ffn,
        gate,
        up,
        hidden,
    )
    return (output, kept)


def layer_backward(grad_rows, encoded, weights, line, kept, buckets):
    (
        gains,
        self_query,
        self_kv,
        self_out,
        cross_query,
        cross_kv,
        cross_out,
        ffn_in,
        ffn_out,
        table,
    ) = weights
    (
        residual,
        after_self,
        after_cross,
        normed_self,
        query,
        keys,
        values,
        mixed,
        normed_cross,
        cross_q,
        cross_k,
        cross_v,
        cross_mixed,
        normed_ffn,
        gate,
        up,
        hidden,
    ) = kept
    count = encoded.shape[0]
    width = grad_rows.shape[1]
    enc_rows = encoded.reshape(-1, width)
    branch = grad_rows.astype(jnp.bfloat16)
    grad_ffn_out = inner_rows(hidden, branch)
    unused, pull = jax.vjp(gated, gate, up)
    grad_gate, grad_up = pull(outer_rows(branch, ffn_out))
    grad_gate = grad_gate.astype(jnp.bfloat16)
    grad_up = grad_up.astype(jnp.bfloat16)
    grad_ffn_in = (inner_rows(normed_ffn, grad_gate), inner_rows(normed_ffn, grad_up))
    grad_normed = outer_rows(grad_gate, ffn_in[0]) + outer_rows(grad_up, ffn_in[1])
    unused, pull = jax.vjp(root_norm, after_cross, gains[2].astype(jnp.float32))
    grad_back, gain_ffn = pull(grad_normed)
    grad_rows = grad_rows + grad_back
    branch = grad_rows.astype(jnp.bfloat16)
    grad_cross_out = inner_rows(cross_mixed, branch)
    grad_mixed = outer_rows(branch, cross_out).astype(jnp.bfloat16)
    grad_cq, grad_ck, grad_cv = attention(
        backward_kernel, (cross_q, cross_k, cross_v, grad_mixed), count
    )
    grad_cross_query = inner_rows(normed_cross, grad_cq)
    grad_cross_kv = (inner_rows(enc_rows, grad_ck), inner_rows(enc_rows, grad_cv))
    grad_states = outer_rows(grad_ck, cross_kv[0]) + outer_rows(grad_cv, cross_kv[1])
    unused, pull = jax.vjp(root_norm, after_self, gains[1].astype(jnp.float32))
    grad_back, gain_cross = pull(outer_rows(grad_cq, cross_query))
    grad_rows = grad_rows + grad_back
    branch = grad_rows.astype(jnp.bfloat16)
    grad_self_out = inner_rows(mixed, branch)
    grad_mixed = outer_rows(branch, self_out).astype(jnp.bfloat16)
    grad_query, grad_keys, grad_values, sums = attention(
        backward_kernel, (query, keys, values, grad_mixed), count, line
    )
    grad_self_query = inner_rows(normed_self, grad_query)
    grad_self_kv = (
        inner_rows(normed_self, grad_keys),
        inner_rows(normed_self, grad_values),
    )
    grad_normed = (
        outer_rows(grad_query, self_query)
        + outer_rows(grad_keys, self_kv[0])
        + outer_rows(grad_values, self_kv[1])
    )
    unused, pull = jax.vjp(root_norm, residual, gains[0].astype(jnp.float32))
    grad_back, gain_self = pull(grad_normed)
    grad_rows = grad_rows + grad_back
    grad_table = table_gradient(jnp.sum(sums, axis=(0, 2)), buckets)
    grads = (
        jnp.stack([gain_self, gain_cross, gain_ffn]),
        grad_self_query,
        grad_self_kv,
        grad_self_out,
        grad_cross_query,
        grad_cross_kv,
        grad_cross_out,
        grad_ffn_in,
        grad_ffn_out,
        grad_table,
    )
    return (grad_rows, grad_states, grads)


def gather_square(stack):
    matrices, piece, width = stack.shape
    if lax.axis_size("rep") == matrices:
        own = lax.dynamic_index_in_dim(stack, lax.axis_index("rep"), 0, keepdims=False)
        whole = lax.all_gather(own, ("rep", "shard"), axis=0, tiled=True)
        return whole.reshape(matrices, -1, width)
    return lax.all_gather(stack, "shard", axis=1, tiled=True)


def gather_weights(
    gains, self_query, self_kv, self_out, cross_query, cross_kv, cross_out, ffn_in, ffn_out, table
):
    small = jnp.concatenate([gains[0].reshape(-1), table.reshape(-1)])
    small = lax.all_gather(small, "shard", axis=0)
    cut = gains[0].size
    all_gains = small[:, :cut].reshape(-1, 3, gains.shape[2]).transpose(1, 0, 2).reshape(3, -1)
    all_table = small[:, cut:].reshape(-1, table.shape[1])
    own = gather_square(jnp.concatenate([self_query, self_kv[0], self_out]))
    cross = gather_square(jnp.concatenate([cross_query, cross_kv[0], cross_out]))
    half = ffn_in.shape[3] // 2
    wide = gather_square(
        jnp.stack([ffn_in[0, m, :, h * half : (h + 1) * half] for m in (0, 1) for h in (0, 1)])
    )
    wide = (
        jnp.concatenate([wide[0], wide[1]], axis=1),
        jnp.concatenate([wide[2], wide[3]], axis=1),
    )
    deep = ffn_out[0].reshape(4, -1, ffn_out.shape[2])
    count = lax.axis_size("shard")
    deep = gather_square(deep)
    deep = deep.reshape(4, count, -1, ffn_out.shape[2]).transpose(1, 0, 2, 3)
    deep = deep.reshape(-1, ffn_out.shape[2])
    return (
        all_gains, own[0], own[1:3], own[3], cross[0], cross[1:3], cross[3], wide, deep, all_table,
    )


def scatter_sum(parts):
    stack = jnp.stack([part.astype(jnp.bfloat16) for part in parts])
    share = lax.psum_scatter(stack, "shard", scatter_dimension=1, tiled=True)
    return lax.psum(share, "rep").astype(jnp.float32)


def reduce_gradients(grads, gains_shape, table_shape):
    (gains, query, kv, out, cross_query, cross_kv, cross_out, ffn_in, ffn_out, table) = grads
    ffn_out = scatter_sum([ffn_out])
    ffn_in = scatter_sum(ffn_in)
    cross = scatter_sum([cross_query, cross_kv[0], cross_kv[1], cross_out])
    own = scatter_sum([query, kv[0], kv[1], out])
    small = lax.psum(
        jnp.concatenate([gains.reshape(-1), table.reshape(-1)]), ("rep", "shard")
    )
    place = lax.axis_index("shard")
    gains = small[: gains.size].reshape(gains.shape)
    table = small[gains.size :].reshape(table.shape)
    gains = lax.dynamic_slice_in_dim(gains, place * gains_shape[2], gains_shape[2], 1)
    table = lax.dynamic_slice_in_dim(table, place * table_shape[0], table_shape[0], 0)
    return (
        gains[None],
        own[0:1],
        own[1:3][None],
        own[3:4],
        cross[0:1],
        cross[1:3][None],
        cross[3:4],
        ffn_in[None],
        ffn_out,
        table,
    )


def shards(
    tokens,
    encoded,
    cotangent,
    buckets,
    gains,
    self_query,
    self_kv,
    self_out,
    cross_query,
    cross_kv,
    cross_out,
    ffn_in,
    ffn_out,
    bias_table,
):
    count, length, width = tokens.shape
    rows = tokens.reshape(-1, width).astype(jnp.float32)
    weights = gather_weights(
        gains, self_query, self_kv, self_out, cross_query, cross_kv, cross_out, ffn_in, ffn_out,
        bias_table,
    )
    line = bias_lines(weights[9], buckets)
    rows, kept = layer_forward(rows, encoded, weights, line)
    grad_rows = cotangent.reshape(-1, width).astype(jnp.float32)
    grad_rows, grad_states, grads = layer_backward(
        grad_rows, encoded, weights, line, kept, buckets
    )
    return (
        rows.astype(jnp.bfloat16).reshape(tokens.shape),
        grad_rows.reshape(tokens.shape),
        grad_states.reshape(encoded.shape),
    ) + reduce_gradients(grads, gains.shape, bias_table.shape)


def solution(mesh):
    return jax.shard_map(
        shards,
        mesh=mesh,
        in_specs=(
            P(("rep", "shard"), None, None),
            P(("rep", "shard"), None, None),
            P(("rep", "shard"), None, None),
            P(),
            P(None, None, "shard"),
            P(None, "shard", None),
            P(None, None, "shard", None),
            P(None, "shard", None),
            P(None, "shard", None),
            P(None, None, "shard", None),
            P(None, "shard", None),
            P(None, None, "shard", None),
            P(None, "shard", None),
            P("shard", None),
        ),
        out_specs=(
            P(("rep", "shard"), None, None),
            P(("rep", "shard"), None, None),
            P(("rep", "shard"), None, None),
            P(None, None, "shard"),
            P(None, "shard", None),
            P(None, None, "shard", None),
            P(None, "shard", None),
            P(None, "shard", None),
            P(None, None, "shard", None),
            P(None, "shard", None),
            P(None, None, "shard", None),
            P(None, "shard", None),
            P("shard", None),
        ),
        check_vma=False,
    )
```

time: 1400 us -> 626 us (0.45)
  local copies, waits for them, and re-layouts: 712 us -> 27.9 us
  matrix products: 120 us -> 66.1 us
  waiting for transfers between devices: 431 us -> 381 us
  Pallas kernels: 0 us -> 46.9 us
  other arithmetic: 43.3 us -> 21.3 us
    gather x2 -> x0, local copies, waits for them, and re-layouts: 530 us -> none  [position_bias(): per_offset[:, jnp.clip(distance, 0, length - 1)]]
    reduce_scatter x7 -> x4, waiting for transfers between devices: 406 us -> 157 us  [scatter_sum(): share = lax.psum_scatter(stack, 'shard', scatter_dimension=1, tiled=True)]
    all_gather x8 -> x4, waiting for transfers between devices: 0.09 us -> 204 us  [gather_square(): whole = lax.all_gather(own, ('rep', 'shard'), axis=0, tiled=True)]
    rev x1, local copies, waits for them, and re-layouts: 54.4 us -> 0.1 us  [table_gradient(): buckets[::-1, None] == jnp.arange(NB)[None, :]]
    unnamed x159 -> x158, local copies, waits for them, and re-layouts: 64.2 us -> 13.3 us
    pallas_call x0 -> x4, Pallas kernels: none -> 46.9 us  [attention(): pl.pallas_call(partial(kernel, line is not None), grid=(count, width // P...]
    dot_general x14 -> x2, matrix products: 36.7 us -> 2.17 us  [the longest x1 1.87 us: table_gradient(): jnp.einsum('ho,ob->bh', sums[:, 1:length + 1], onehot, precision=highest)]
    reshape x1 -> x7, local copies, waits for them, and re-layouts: 30.8 us -> 1.76 us  [the longest x1 1.4 us: reduce_gradients(): table.reshape(-1)]
  transfers between devices with their start and end apart: 18 -> 9, of which waited for: 8 -> 8; matrix products, arithmetic and copies ran while one was open for 58% -> 13% of each run, Pallas kernels for 0% -> 8%
where the time goes in v1:
time: 626 us; the launch traced here: 616 us
  waiting for transfers between devices  381 us (61%)
  matrix products  66.1 us (11%)
  blocking collectives  56.4 us (9%)
  Pallas kernels  46.9 us (7%)
  local copies, waits for them, and re-layouts  27.9 us (4%)
  other arithmetic  21.3 us (3%)
  between operations  15.7 us (3%)
    all_gather x4, waiting for transfers between devices, gather_square(): whole = lax.all_gather(own, ('rep', 'shard'), axis=0, tiled=True)  204 us
    reduce_scatter x4, waiting for transfers between devices, scatter_sum(): share = lax.psum_scatter(stack, 'shard', scatter_dimension=1, tiled=True)  157 us
    pallas_call x4, Pallas kernels, attention(): pl.pallas_call(partial(kernel, line is not None), grid=(count, width // P...  46.9 us
    psum x1, blocking collectives, reduce_gradients(): lax.psum(jnp.concatenate([gains.reshape(-1), table.reshape(-1)]), ('rep',...  38 us
    dot_general x11, matrix products, outer_rows(): lax.dot_general(left, right, (((1,), (1,)), ((), ())), preferred_element_...  28.5 us
    dot_general x11, matrix products, product(): return jnp.dot(left, right, preferred_element_type=jnp.float32)  20.4 us
    psum x1, waiting for transfers between devices, scatter_sum(): return lax.psum(share, 'rep').astype(jnp.float32)  19.5 us
    unnamed x1, blocking collectives  18.4 us
  transfers between devices with their start and end apart: 9, of which 8 were waited for; matrix products, arithmetic and copies ran while one was open for 13% of the time, Pallas kernels for 8%

profile of v1, /device:TPU:0, one launch (start us, length us, event | category | flops | bytes accessed | tf_op | source)
XLA Modules:
  0.0 616.1 jit_solution(5812601322484684370)
XLA Ops:
  7.3 1.7 constant_dynamic-slice_fusion.2
  9.0 1.7 fusion.60
  15.0 18.4 %all-reduce = bf16[2688]{0:T(1024)(128)(2,1)S(1)} all-reduce(bf16[2688]{0:T(1024)(128)(2,1)S(1)} %dynamic-update-slice), channel_id=2, replica_groups=mesh['rep'=4,'shard'=8] {'shard'}, use_global_device_ids=true, to_apply=%add | all-reduce | flops 2688 | bytes 10752
  35.4 38.1 %all-gather.16.cloned.1.call-done = bf16[1,2048,768]{2,1,0:T(8,128)(2,1)} async-done(((bf16[1,64,768]{2,1,0:T(8,128)(2,1)}), bf16[1,2048,768]{2,1,0:T(8,128)(2,1)}) %all-gather.16.cloned.1.call-update) | async-done | bytes 3145744 | tf_op jit(solution)/shard_map/all_gather | solution.py:330
  73.5 2.3 copy.40
  75.8 1.6 copy-done.32
  77.4 3.1 fusion.42
  80.5 59.1 %all-gather.10.cloned.1.call-done = bf16[1,3072,768]{2,1,0:T(8,128)(2,1)} async-done(((bf16[1,96,768]{2,1,0:T(8,128)(2,1)}), bf16[1,3072,768]{2,1,0:T(8,128)(2,1)}) %all-gather.10.cloned.1.call-update) | async-done | bytes 4718608 | tf_op jit(solution)/shard_map/all_gather | solution.py:330
  139.6 2.1 convolution_convert_fusion.16.query_ref
  141.8 2.2 convolution_convert_fusion.15.keys_ref
  144.8 12.0 %shard_map.237 = bf16[384,768]{1,0:T(8,128)(2,1)S(1)} custom-call(bf16[384,768]{1,0:T(8,128)(2,1)S(1)} %convolution_convert_fusion.16.query_ref, bf16[384,768]{1,0:T(8,128)(2,1)S(1)} %convolution_convert_fusion.15.keys_ref, bf16[384,768]{1,0:T(8,128)(2,1)S(1)} %convolution_convert_fusion.14.values_ref, f32[12,1,768]{2,1,0:T(1,128)S(1)} %broadcast_in_dim.62.refs_0_), custom_call_target="tpu_custom_call" | custom-call | flops 452984832 | bytes 3538944 | tf_op jit(solution)/shard_map/pallas_call | solution.py:145
  157.5 48.3 %all-gather.12.cloned.1.call-done = bf16[1,3072,768]{2,1,0:T(8,128)(2,1)} async-done(((bf16[1,96,768]{2,1,0:T(8,128)(2,1)}), bf16[1,3072,768]{2,1,0:T(8,128)(2,1)}) %all-gather.12.cloned.1.call-update) | async-done | bytes 4718608 | tf_op jit(solution)/shard_map/all_gather | solution.py:330
  205.8 1.9 fusion.28.keys_ref
  207.7 1.9 fusion.29.values_ref
  210.3 6.4 %shard_map.238 = bf16[384,768]{1,0:T(8,128)(2,1)S(1)} custom-call(bf16[384,768]{1,0:T(8,128)(2,1)S(1)} %convolution_convert_fusion.13.query_ref, bf16[256,768]{1,0:T(8,128)(2,1)S(1)} %fusion.28.keys_ref, bf16[256,768]{1,0:T(8,128)(2,1)S(1)} %fusion.29.values_ref), custom_call_target="tpu_custom_call" | custom-call | flops 301989888 | bytes 2752512 | tf_op jit(solution)/shard_map/pallas_call | solution.py:145
  219.5 58.1 %all-gather.14.cloned.1.call-done = bf16[1,3072,1024]{2,1,0:T(8,128)(2,1)} async-done(((bf16[1,96,1024]{2,1,0:T(8,128)(2,1)}), bf16[1,3072,1024]{2,1,0:T(8,128)(2,1)}) %all-gather.14.cloned.1.call-update) | async-done | bytes 6291472 | tf_op jit(solution)/shard_map/all_gather | solution.py:330
  277.6 3.6 slice_bitcast_fusion.3
  281.3 1.4 fusion.11
  285.3 5.9 fusion.3
  291.3 1.2 copy-done.72
  292.5 3.5 fusion.9
  296.5 3.9 fusion.10
  300.5 3.8 multiply_reduce_fusion
  306.4 11.8 %shard_map.239 = (bf16[384,768]{1,0:T(8,128)(2,1)S(1)}, bf16[256,768]{1,0:T(8,128)(2,1)S(1)}, bf16[256,768]{1,0:T(8,128)(2,1)S(1)}) custom-call(bf16[384,768]{1,0:T(8,128)(2,1)S(1)} %copy-done.10, bf16[256,768]{1,0:T(8,128)(2,1)S(1)} %copy-done.12, bf16[256,768]{1,0:T(8,128)(2,1)S(1)} %copy-done.14, bf16[384,768]{1,0:T(8,128)(2,1)S(1)} %convolution_convert_fusion.12.upstream_ref), custom_call_target="tpu_custom_call" | custom-call | flops 754974720 | bytes 3932160 | tf_op jit(solution)/shard_map/pallas_call | solution.py:145
  318.3 1.4 multiply_reduce_fusion.1
  320.1 2.4 convolution_convert_fusion.11.upstream_ref
  322.6 16.7 %shard_map.240 = (bf16[384,768]{1,0:T(8,128)(2,1)S(1)}, bf16[384,768]{1,0:T(8,128)(2,1)S(1)}, bf16[384,768]{1,0:T(8,128)(2,1)S(1)}, f32[1,12,1,768]{3,2,1,0:T(1,128)S(1)}) custom-call(bf16[384,768]{1,0:T(8,128)(2,1)S(1)} %copy-done.16, bf16[384,768]{1,0:T(8,128)(2,1)S(1)} %copy-done.18, bf16[384,768]{1,0:T(8,128)(2,1)S(1)} %copy-done.20, ...), custom_call_target="tpu_custom_call" | custom-call | flops 1132462080 | bytes 4718592 | tf_op jit(solution)/shard_map/pallas_call | solution.py:145
  343.0 2.4 pad_maximum_fusion.1
  349.5 2.5 pad_maximum_fusion.2
  353.1 3.4 fusion.8
  356.5 1.8 fusion.7
  358.3 3.2 pad_maximum_fusion
  362.9 1.9 fusion.38
  364.9 2.9 convolution_add_fusion.1
  367.8 31.3 %reduce-scatter.5.cloned.1.call-done = bf16[4,96,768]{2,1,0:T(8,128)(2,1)} async-done(((bf16[4,768,768]{2,1,0:T(8,128)(2,1)}), bf16[4,96,768]{2,1,0:T(8,128)(2,1)}) %reduce-scatter.5.cloned.1.call-update) | async-done | bytes 589840 | tf_op jit(solution)/shard_map/reduce_scatter | solution.py:365
  399.2 55.6 %reduce-scatter.7.cloned.1.call-done = bf16[4,96,768]{2,1,0:T(8,128)(2,1)} async-done(((bf16[4,768,768]{2,1,0:T(8,128)(2,1)}), bf16[4,96,768]{2,1,0:T(8,128)(2,1)}) %reduce-scatter.7.cloned.1.call-update) | async-done | bytes 589840 | tf_op jit(solution)/shard_map/reduce_scatter | solution.py:365
  454.8 70.5 %reduce-scatter.9.cloned.1.call-done = bf16[2,96,2048]{2,1,0:T(8,128)(2,1)} async-done(((bf16[2,768,2048]{2,1,0:T(8,128)(2,1)}), bf16[2,96,2048]{2,1,0:T(8,128)(2,1)}) %reduce-scatter.9.cloned.1.call-update) | async-done | bytes 786448 | tf_op jit(solution)/shard_map/reduce_scatter | solution.py:365
  525.3 1.9 fusion.61
  527.2 1.4 reshape.220
  529.3 3.6 fusion.31
  533.7 38.0 %psum.35 = f32[2688]{0:T(1024)S(1)} all-reduce(f32[2688]{0:T(1024)S(1)} %pad_maximum_fusion.12), channel_id=1, replica_groups=mesh['rep'=4,'shard'=8] {'rep','shard'}, use_global_device_ids=true, to_apply=%region_9.10 | all-reduce | flops 2688 | bytes 21504 | tf_op jit(solution)/shard_map/psum | solution.py:375
  573.8 1.9 fusion.40
  575.7 2.8 fusion.26
  578.5 2.2 fusion.35
  580.7 2.2 fusion.27
  582.9 19.5 %all-reduce.4.cloned.1.call-done = (bf16[4,96,768]{2,1,0:T(8,128)(2,1)}, bf16[4,96,768]{2,1,0:T(8,128)(2,1)}, bf16[1,2,96,2048]{3,2,1,0:T(8,128)(2,1)}, bf16[1,256,768]{2,1,0:T(8,128)(2,1)}) async-done(((bf16[4,96,768]{2,1,0:T(8,128)(2,1)}, bf16[4,96,768]{2,1,0:T(8,128)(2,1)}, bf16[1,2,96,2048]{3,2,1,0:T(8,128)(2,1)}, bf16[1,256,768]{2,1,0:T(8,128)(2,1)}), (bf16[4,96,768]{2,1,0:T(8,128)(2,1)}, ...) | async-done | bytes 2359312 | tf_op jit(solution)/shard_map/psum | solution.py:366
  602.4 1.2 convert_element_type.189
  606.0 1.3 broadcast_in_dim.70
  (237 shorter events, 34.1 us)
Async XLA Ops:
  7.2 198.6 %copy-start = (bf16[1,256,768]{2,1,0:T(8,128)(2,1)S(1)}, bf16[1,256,768]{2,1,0:T(8,128)(2,1)}, u32[]{:S(2)}) copy-start(bf16[1,256,768]{2,1,0:T(8,128)(2,1)} %param.15) | copy-start | bytes 1179652
  7.2 3.6 copy-start.58
  7.2 3.6 copy-start.57
  7.2 3.6 copy-start.59
  7.2 4.5 copy-start.49
  7.2 66.3 %all-gather.16.cloned.1.call-start = ((), (), s32[]{:S(2)}) async-start(), calls=%async_computation.11 | async-start | bytes 3244032 | tf_op jit(solution)/shard_map/all_gather | solution.py:330
  9.0 130.7 %all-gather.10.cloned.1.call-start = ((), (), s32[]{:S(2)}) async-start(), calls=%async_computation.8 | async-start | bytes 4866048 | tf_op jit(solution)/shard_map/all_gather | solution.py:330
  10.7 195.0 %all-gather.12.cloned.1.call-start = ((), (), s32[]{:S(2)}) async-start(), calls=%async_computation.9 | async-start | bytes 4866048 | tf_op jit(solution)/shard_map/all_gather | solution.py:330
  11.6 266.0 %all-gather.14.cloned.1.call-start = ((), (), s32[]{:S(2)}) async-start(), calls=%async_computation.10 | async-start | bytes 6488064 | tf_op jit(solution)/shard_map/all_gather | solution.py:330
  11.8 23.5 %copy-start.37 = (bf16[1,384,768]{2,1,0:T(8,128)(2,1)S(1)}, bf16[1,384,768]{2,1,0:T(8,128)(2,1)}, u32[]{:S(2)}) copy-start(bf16[1,384,768]{2,1,0:T(8,128)(2,1)} %param.14) | copy-start | bytes 1769476
  12.6 355.2 %reduce-scatter.11.cloned.1.call-start = ((), (), s32[]{:S(2)}) async-start(), calls=%async_computation.7 | async-start | bytes 3538944 | tf_op jit(solution)/shard_map/reduce_scatter | solution.py:365
  35.1 109.6 %copy-start.3 = (f32[12,1,768]{2,1,0:T(1,128)}, f32[12,1,768]{2,1,0:T(1,128)S(1)}, u32[]{:S(2)}) copy-start(f32[12,1,768]{2,1,0:T(1,128)S(1)} %broadcast_in_dim.62.refs_0_) | copy-start | bytes 110596
  35.4 108.5 %copy-start.60 = (f32[384]{0:T(512)}, f32[384]{0:T(512)S(1)}, u32[]{:S(2)}) copy-start(f32[384]{0:T(512)S(1)} %fusion.69) | copy-start | bytes 4612
  73.5 3.9 copy-start.51
  139.6 4.3 copy-start.34
  141.7 2.9 copy-start.15
  144.7 12.0 %copy-start.19 = (bf16[384,768]{1,0:T(8,128)(2,1)}, bf16[384,768]{1,0:T(8,128)(2,1)S(1)}, u32[]{:S(2)}) copy-start(bf16[384,768]{1,0:T(8,128)(2,1)S(1)} %convolution_convert_fusion.14.values_ref) | copy-start | bytes 1769476
  144.7 12.0 %copy-start.38 = (bf16[1,384,768]{2,1,0:T(8,128)(2,1)S(1)}, bf16[1,384,768]{2,1,0:T(8,128)(2,1)}, u32[]{:S(2)}) copy-start(bf16[1,384,768]{2,1,0:T(8,128)(2,1)} %param.14) | copy-start | bytes 1769476
  157.5 50.2 %copy-start.62 = (f32[384]{0:T(512)}, f32[384]{0:T(512)S(1)}, u32[]{:S(2)}) copy-start(f32[384]{0:T(512)S(1)} %get-tuple-element.55) | copy-start | bytes 4612
  157.5 59.2 %copy-start.25 = (f32[384,768]{1,0:T(8,128)}, f32[384,768]{1,0:T(8,128)S(1)}, u32[]{:S(2)}) copy-start(f32[384,768]{1,0:T(8,128)S(1)} %get-tuple-element.56) | copy-start | bytes 3538948
  205.8 3.8 copy-start.31
  210.3 6.4 %copy-start.9 = (bf16[384,768]{1,0:T(8,128)(2,1)}, bf16[384,768]{1,0:T(8,128)(2,1)S(1)}, u32[]{:S(2)}) copy-start(bf16[384,768]{1,0:T(8,128)(2,1)S(1)} %convolution_convert_fusion.13.query_ref) | copy-start | bytes 1769476
  277.6 3.7 copy-start.54
  281.2 3.1 copy-start.43
  281.3 4.1 copy-start.70
  285.3 7.1 %copy-start.52 = (bf16[1,384,768]{2,1,0:T(8,128)(2,1)S(1)}, bf16[1,384,768]{2,1,0:T(8,128)(2,1)}, u32[]{:S(2)}) copy-start(bf16[1,384,768]{2,1,0:T(8,128)(2,1)} %param.16) | copy-start | bytes 1769476
  296.0 103.2 %reduce-scatter.5.cloned.1.call-start = ((), (), s32[]{:S(2)}) async-start(), calls=%async_computation.4 | async-start | bytes 5308416 | tf_op jit(solution)/shard_map/reduce_scatter | solution.py:365
  296.4 4.0 copy-start.29
  296.5 4.0 copy-start.42
  296.5 4.0 copy-start.44
  296.5 8.2 %slice-start = ((s8[4718592]{0:T(1024)(128)(4,1)}), s8[4194304]{0:T(1024)(128)(4,1)S(1)}, s32[]{:S(2)}) async-start(s8[4718592]{0:T(1024)(128)(4,1)} %bitcast.177), calls=%async_computation.13 | async-start | bytes 8388608
  300.4 3.9 copy-start.53
  300.5 4.2 slice-start.1
  304.7 15.0 %copy-start.23 = (f32[384,768]{1,0:T(8,128)}, f32[384,768]{1,0:T(8,128)S(1)}, u32[]{:S(2)}) copy-start(f32[384,768]{1,0:T(8,128)S(1)} %fusion.32) | copy-start | bytes 3538948
  306.4 11.9 %copy-start.26 = (f32[384,768]{1,0:T(8,128)S(1)}, f32[384,768]{1,0:T(8,128)}, u32[]{:S(2)}) copy-start(f32[384,768]{1,0:T(8,128)} %copy-done.25) | copy-start | bytes 3538948
  320.0 22.2 %copy-start.21 = (f32[384,768]{1,0:T(8,128)}, f32[384,768]{1,0:T(8,128)S(1)}, u32[]{:S(2)}) copy-start(f32[384,768]{1,0:T(8,128)S(1)} %fusion.33) | copy-start | bytes 3538948
  322.5 16.8 %copy-start.39 = (bf16[1,384,768]{2,1,0:T(8,128)(2,1)S(1)}, bf16[1,384,768]{2,1,0:T(8,128)(2,1)}, u32[]{:S(2)}) copy-start(bf16[1,384,768]{2,1,0:T(8,128)(2,1)} %param.14) | copy-start | bytes 1769476
  322.5 16.8 %copy-start.61 = (f32[384]{0:T(512)S(1)}, f32[384]{0:T(512)}, u32[]{:S(2)}) copy-start(f32[384]{0:T(512)} %copy-done.60) | copy-start | bytes 4612
  345.5 109.3 %reduce-scatter.7.cloned.1.call-start = ((), (), s32[]{:S(2)}) async-start(), calls=%async_computation.5 | async-start | bytes 5308416 | tf_op jit(solution)/shard_map/reduce_scatter | solution.py:365
  352.1 173.2 %reduce-scatter.9.cloned.1.call-start = ((), (), s32[]{:S(2)}) async-start(), calls=%async_computation.6 | async-start | bytes 7077888 | tf_op jit(solution)/shard_map/reduce_scatter | solution.py:365
  353.1 3.4 copy-start.71
  361.6 240.9 %all-reduce.4.cloned.1.call-start = ((), (), s32[]{:S(2)}) async-start(), calls=%async_computation.12 | async-start | bytes 4718592 | tf_op jit(solution)/shard_map/psum | solution.py:366
  525.3 3.3 copy-start.66
  525.3 4.0 copy-start.8
  525.3 4.0 copy-start.40
  525.3 4.0 copy-start.47
  573.8 4.7 copy-start.48
  575.6 5.0 copy-start.33
  (37 other events, 58.6 us)
Sparse Core Ops, SparseCore 0:
  11.6 61.8 all-gather.15
  77.1 62.4 all-gather.9
  143.2 62.4 all-gather.11
  209.2 68.3 all-gather.13
  296.1 38.8 reduce-scatter.10
  345.6 53.5 reduce-scatter.4
  401.5 53.2 reduce-scatter.6
  457.1 68.1 reduce-scatter.8
  528.7 73.7 all-reduce.3

commit v2 on v1

--- a/solution.py
+++ b/solution.py
@@ -335,26 +335,42 @@
 def gather_weights(
     gains, self_query, self_kv, self_out, cross_query, cross_kv, cross_out, ffn_in, ffn_out, table
 ):
+    width = self_query.shape[2]
     small = jnp.concatenate([gains[0].reshape(-1), table.reshape(-1)])
-    small = lax.all_gather(small, "shard", axis=0)
-    cut = gains[0].size
-    all_gains = small[:, :cut].reshape(-1, 3, gains.shape[2]).transpose(1, 0, 2).reshape(3, -1)
-    all_table = small[:, cut:].reshape(-1, table.shape[1])
-    own = gather_square(jnp.concatenate([self_query, self_kv[0], self_out]))
-    cross = gather_square(jnp.concatenate([cross_query, cross_kv[0], cross_out]))
+    small = jnp.pad(small, (0, 16 * width - small.size)).reshape(1, 16, width)
+    own = jnp.concatenate([self_query, self_kv[0], self_out])
+    cross = jnp.concatenate([cross_query, cross_kv[0], cross_out])
     half = ffn_in.shape[3] // 2
-    wide = gather_square(
-        jnp.stack([ffn_in[0, m, :, h * half : (h + 1) * half] for m in (0, 1) for h in (0, 1)])
-    )
+    rest = half - width
+    folds = width // rest
+    piece = ffn_in.shape[2]
+    wide = [ffn_in[0, m, :, h * half : (h + 1) * half] for m in (0, 1) for h in (0, 1)]
+    most = jnp.stack([item[:, :width] for item in wide])
+    last = jnp.stack([item[:, width:] for item in wide]).reshape(4, folds, -1, rest)
+    last = jnp.concatenate([last[:, fold] for fold in range(folds)], axis=2)
+    deep = ffn_out[0].reshape(4, -1, width)
+    blocks = [own, cross, most, last, deep, jnp.broadcast_to(small, (4, 16, width))]
+    count = lax.axis_size("shard")
+    every = gather_square(jnp.concatenate(blocks, axis=1)).reshape(4, count, -1, width)
+    cuts, start = [], 0
+    for block in blocks:
+        cuts.append(every[:, :, start : start + block.shape[1]])
+        start += block.shape[1]
+    own = cuts[0].reshape(4, -1, width)
+    cross = cuts[1].reshape(4, -1, width)
+    last = jnp.concatenate(
+        [cuts[3][..., fold * rest : (fold + 1) * rest] for fold in range(folds)], axis=2
+    )
+    wide = jnp.concatenate([cuts[2], last], axis=3).reshape(4, count * piece, half)
     wide = (
         jnp.concatenate([wide[0], wide[1]], axis=1),
         jnp.concatenate([wide[2], wide[3]], axis=1),
     )
-    deep = ffn_out[0].reshape(4, -1, ffn_out.shape[2])
-    count = lax.axis_size("shard")
-    deep = gather_square(deep)
-    deep = deep.reshape(4, count, -1, ffn_out.shape[2]).transpose(1, 0, 2, 3)
-    deep = deep.reshape(-1, ffn_out.shape[2])
+    deep = cuts[4].transpose(1, 0, 2, 3).reshape(-1, width)
+    small = cuts[5][0].reshape(count, -1)
+    cut = gains[0].size
+    all_gains = small[:, :cut].reshape(count, 3, -1).transpose(1, 0, 2).reshape(3, -1)
+    all_table = small[:, cut : cut + table.size].reshape(-1, table.shape[1])
     return (
         all_gains, own[0], own[1:3], own[3], cross[0], cross[1:3], cross[3], wide, deep, all_table,
     )

time: 626 us -> 549 us (0.88)
  waiting for transfers between devices: 381 us -> 309 us
  local copies, waits for them, and re-layouts: 27.9 us -> 55.3 us
  blocking collectives: 56.4 us -> 38.4 us
  matrix products: 66.1 us -> 50.7 us
    all_gather x4 -> x1, waiting for transfers between devices: 204 us -> 127 us  [gather_square(): whole = lax.all_gather(own, ('rep', 'shard'), axis=0, tiled=True)]
    unnamed x1 -> x0, blocking collectives: 18.4 us -> none
    slice x1 -> x10, local copies, waits for them, and re-layouts: 0.07 us -> 16.9 us  [the longest x1 6.96 us: gather_weights(): cross[3]]
    unnamed x158 -> x186, local copies, waits for them, and re-layouts: 13.3 us -> 24.7 us
    dot_general x11, matrix products: 28.5 us -> 18.1 us  [outer_rows(): lax.dot_general(left, right, (((1,), (1,)), ((), ())), preferred_element_...]
  transfers between devices with their start and end apart: 9 -> 6, of which waited for: 8 -> 5; matrix products, arithmetic and copies ran while one was open for 13% -> 9% of each run, Pallas kernels for 8% -> 5%
where the time goes in v2:
time: 549 us; the launch traced here: 538 us
  waiting for transfers between devices  309 us (56%)
  local copies, waits for them, and re-layouts  55.3 us (10%)
  matrix products  50.7 us (9%)
  Pallas kernels  47 us (9%)
  blocking collectives  38.4 us (7%)
  other arithmetic  21.1 us (4%)
  between operations  15.8 us (3%)
    reduce_scatter x4, waiting for transfers between devices, scatter_sum(): share = lax.psum_scatter(stack, 'shard', scatter_dimension=1, tiled=True)  159 us
    all_gather x1, waiting for transfers between devices, gather_square(): whole = lax.all_gather(own, ('rep', 'shard'), axis=0, tiled=True)  127 us
    pallas_call x4, Pallas kernels, attention(): pl.pallas_call(partial(kernel, line is not None), grid=(count, width // P...  47 us
    psum x1, blocking collectives, reduce_gradients(): lax.psum(jnp.concatenate([gains.reshape(-1), table.reshape(-1)]), ('rep',...  38.4 us
    unnamed x186, local copies, waits for them, and re-layouts  24.7 us
    psum x1, waiting for transfers between devices, scatter_sum(): return lax.psum(share, 'rep').astype(jnp.float32)  23.5 us
    dot_general x11, matrix products, outer_rows(): lax.dot_general(left, right, (((1,), (1,)), ((), ())), preferred_element_...  18.1 us
    dot_general x11, matrix products, product(): return jnp.dot(left, right, preferred_element_type=jnp.float32)  16.2 us
  transfers between devices with their start and end apart: 6, of which 5 were waited for; matrix products, arithmetic and copies ran while one was open for 9% of the time, Pallas kernels for 5%

profile of v2, /device:TPU:0, one launch (start us, length us, event | category | flops | bytes accessed | tf_op | source)
XLA Modules:
  0.0 538.1 jit_solution(14042222454250296332)
XLA Ops:
  7.2 1.3 slice_bitcast_fusion.7
  13.3 1.3 pad_add_fusion
  16.0 127.1 %all-gather.3.cloned.1.call-done = bf16[1,12800,768]{2,1,0:T(8,128)(2,1)} async-done(((bf16[1,400,768]{2,1,0:T(8,128)(2,1)}), bf16[1,12800,768]{2,1,0:T(8,128)(2,1)}) %all-gather.3.cloned.1.call-update) | async-done | bytes 19660816 | tf_op jit(solution)/shard_map/all_gather | solution.py:330
  143.1 0.9 slice_bitcast_fusion.3
  144.8 2.6 fusion.83
  147.3 2.1 slice_bitcast_fusion
  149.4 4.8 slice.273
  154.3 7.0 %fusion.84 = (bf16[1,8,96,768]{3,2,1,0:T(8,128)(2,1)}, bf16[1,8,96,768]{3,2,1,0:T(8,128)(2,1)}, bf16[1,8,96,768]{3,2,1,0:T(8,128)(2,1)}, bf16[1,8,96,768]{3,2,1,...) fusion(bf16[4,8,400,768]{3,2,1,0:T(8,128)(2,1)} %bitcast.205), kind=kLoop, calls=%fused_computation.172 | loop fusion | bytes 18874368 | tf_op jit(solution)/shard_map/slice | solution.py:375
  163.5 1.4 reshape.262
  164.9 1.0 convolution_select_fusion
  166.2 3.2 copy-done.22
  169.9 4.8 maximum_maximum_fusion
  174.7 1.1 fusion.85
  176.5 1.6 copy-done.31
  178.6 1.2 copy-done.44
  183.2 11.8 %shard_map.237 = bf16[384,768]{1,0:T(8,128)(2,1)S(1)} custom-call(bf16[384,768]{1,0:T(8,128)(2,1)S(1)} %convolution_convert_fusion.16.query_ref, bf16[384,768]{1,0:T(8,128)(2,1)S(1)} %convolution_convert_fusion.15.keys_ref, bf16[384,768]{1,0:T(8,128)(2,1)S(1)} %convolution_convert_fusion.14.values_ref, f32[12,1,768]{2,1,0:T(1,128)S(1)} %broadcast_in_dim.71.refs_0_), custom_call_target="tpu_custom_call" | custom-call | flops 452984832 | bytes 3538944 | tf_op jit(solution)/shard_map/pallas_call | solution.py:145
  197.0 6.4 %shard_map.238 = bf16[384,768]{1,0:T(8,128)(2,1)S(1)} custom-call(bf16[384,768]{1,0:T(8,128)(2,1)S(1)} %convolution_convert_fusion.13.query_ref, bf16[256,768]{1,0:T(8,128)(2,1)S(1)} %fusion.33.keys_ref, bf16[256,768]{1,0:T(8,128)(2,1)S(1)} %fusion.34.values_ref), custom_call_target="tpu_custom_call" | custom-call | flops 301989888 | bytes 2752512 | tf_op jit(solution)/shard_map/pallas_call | solution.py:145
  204.5 1.4 fusion.47
  206.1 1.4 fusion.11
  207.5 6.1 %fusion.3 = (bf16[384,2048]{1,0:T(8,128)(2,1)}, bf16[384,2048]{1,0:T(8,128)(2,1)}, bf16[384,2048]{1,0:T(8,128)(2,1)S(1)}) fusion(f32[384,2048]{1,0:T(8,128)S(1)} %fusion.11, f32[2048,384]{0,1:T(8,128)S(1)} %fusion.47, bf16[384,768]{1,0:T(8,128)(2,1)S(1)} %multiply_convert_fusion.1, bf16[768,1024]{1,0:T(8,128)(2,1)S(1)} %bitcast.226, ...), kind=kOutput, calls=%fused_computation.14 | convolution fusion | flops 1237843968 | bytes 14745600 | tf_op jit(solution)/shard_map/dot_general | solution.py:35
  213.7 1.2 copy-done.89
  214.8 3.5 fusion.9
  218.5 3.9 fusion.10
  222.6 2.1 multiply_reduce_fusion
  225.1 0.9 copy-done.36
  227.6 12.0 %shard_map.239 = (bf16[384,768]{1,0:T(8,128)(2,1)S(1)}, bf16[256,768]{1,0:T(8,128)(2,1)S(1)}, bf16[256,768]{1,0:T(8,128)(2,1)S(1)}) custom-call(bf16[384,768]{1,0:T(8,128)(2,1)S(1)} %convolution_convert_fusion.13.query_ref, bf16[256,768]{1,0:T(8,128)(2,1)S(1)} %copy-done.8, bf16[256,768]{1,0:T(8,128)(2,1)S(1)} %copy-done.6, ...), custom_call_target="tpu_custom_call" | custom-call | flops 754974720 | bytes 3932160 | tf_op jit(solution)/shard_map/pallas_call | solution.py:145
  239.7 1.3 multiply_reduce_fusion.1
  241.3 1.0 copy-done.34
  244.2 16.7 %shard_map.240 = (bf16[384,768]{1,0:T(8,128)(2,1)S(1)}, bf16[384,768]{1,0:T(8,128)(2,1)S(1)}, bf16[384,768]{1,0:T(8,128)(2,1)S(1)}, f32[1,12,1,768]{3,2,1,0:T(1,128)S(1)}) custom-call(bf16[384,768]{1,0:T(8,128)(2,1)S(1)} %copy-done.18, bf16[384,768]{1,0:T(8,128)(2,1)S(1)} %copy-done.16, bf16[384,768]{1,0:T(8,128)(2,1)S(1)} %copy-done.14, ...), custom_call_target="tpu_custom_call" | custom-call | flops 1132462080 | bytes 4718592 | tf_op jit(solution)/shard_map/pallas_call | solution.py:145
  264.7 2.5 pad_maximum_fusion.1
  271.2 2.4 pad_maximum_fusion.2
  274.7 3.3 fusion.7
  278.0 1.8 fusion.8
  279.9 3.2 pad_maximum_fusion
  286.0 1.7 convolution_add_fusion.1
  287.7 32.8 %reduce-scatter.5.cloned.1.call-done = bf16[4,96,768]{2,1,0:T(8,128)(2,1)} async-done(((bf16[4,768,768]{2,1,0:T(8,128)(2,1)}), bf16[4,96,768]{2,1,0:T(8,128)(2,1)}) %reduce-scatter.5.cloned.1.call-update) | async-done | bytes 589840 | tf_op jit(solution)/shard_map/reduce_scatter | solution.py:381
  320.5 55.5 %reduce-scatter.7.cloned.1.call-done = bf16[4,96,768]{2,1,0:T(8,128)(2,1)} async-done(((bf16[4,768,768]{2,1,0:T(8,128)(2,1)}), bf16[4,96,768]{2,1,0:T(8,128)(2,1)}) %reduce-scatter.7.cloned.1.call-update) | async-done | bytes 589840 | tf_op jit(solution)/shard_map/reduce_scatter | solution.py:381
  376.0 70.4 %reduce-scatter.9.cloned.1.call-done = bf16[2,96,2048]{2,1,0:T(8,128)(2,1)} async-done(((bf16[2,768,2048]{2,1,0:T(8,128)(2,1)}), bf16[2,96,2048]{2,1,0:T(8,128)(2,1)}) %reduce-scatter.9.cloned.1.call-update) | async-done | bytes 786448 | tf_op jit(solution)/shard_map/reduce_scatter | solution.py:381
  446.4 3.7 fusion.35
  450.6 38.4 %psum.35 = f32[2688]{0:T(1024)S(1)} all-reduce(f32[2688]{0:T(1024)S(1)} %pad_maximum_fusion.13), channel_id=1, replica_groups=mesh['rep'=4,'shard'=8] {'rep','shard'}, use_global_device_ids=true, to_apply=%region_9.10 | all-reduce | flops 2688 | bytes 21504 | tf_op jit(solution)/shard_map/psum | solution.py:391
  491.8 1.4 fusion.31
  494.1 1.3 fusion.44
  495.8 3.6 fusion.32
  499.5 23.5 %all-reduce.4.cloned.1.call-done = (bf16[4,96,768]{2,1,0:T(8,128)(2,1)}, bf16[4,96,768]{2,1,0:T(8,128)(2,1)}, bf16[1,2,96,2048]{3,2,1,0:T(8,128)(2,1)}, bf16[1,256,768]{2,1,0:T(8,128)(2,1)}) async-done(((bf16[4,96,768]{2,1,0:T(8,128)(2,1)}, bf16[4,96,768]{2,1,0:T(8,128)(2,1)}, bf16[1,2,96,2048]{3,2,1,0:T(8,128)(2,1)}, bf16[1,256,768]{2,1,0:T(8,128)(2,1)}), (bf16[4,96,768]{2,1,0:T(8,128)(2,1)}, ...) | async-done | bytes 2359312 | tf_op jit(solution)/shard_map/psum | solution.py:382
  523.0 1.9 fusion.87
  524.9 1.0 copy-done.52
  528.6 1.3 broadcast_in_dim.79
  529.9 0.9 convert_element_type.210
  (272 shorter events, 40.3 us)
Async XLA Ops:
  7.2 168.7 %copy-start = (bf16[1,256,768]{2,1,0:T(8,128)(2,1)S(1)}, bf16[1,256,768]{2,1,0:T(8,128)(2,1)}, u32[]{:S(2)}) copy-start(bf16[1,256,768]{2,1,0:T(8,128)(2,1)} %param.15) | copy-start | bytes 1179652
  7.2 135.9 %all-gather.3.cloned.1.call-start = ((), (), s32[]{:S(2)}) async-start(), calls=%async_computation.8 | async-start | bytes 20275200 | tf_op jit(solution)/shard_map/all_gather | solution.py:330
  11.0 3.6 copy-start.40
  11.9 275.8 %reduce-scatter.11.cloned.1.call-start = ((), (), s32[]{:S(2)}) async-start(), calls=%async_computation.7 | async-start | bytes 3538944 | tf_op jit(solution)/shard_map/reduce_scatter | solution.py:381
  165.9 17.2 %copy-start.11 = (f32[12,1,768]{2,1,0:T(1,128)}, f32[12,1,768]{2,1,0:T(1,128)S(1)}, u32[]{:S(2)}) copy-start(f32[12,1,768]{2,1,0:T(1,128)S(1)} %broadcast_in_dim.71.refs_0_) | copy-start | bytes 110596
  165.9 3.5 copy-start.22
  166.0 3.6 copy-start.54
  166.0 3.7 copy-start.55
  166.0 3.9 copy-start.56
  166.2 38.0 %copy-start.50 = (bf16[8,4,64,768]{3,2,1,0:T(8,128)(2,1)}, bf16[8,4,64,768]{3,2,1,0:T(8,128)(2,1)S(1)}, u32[]{:S(2)}) copy-start(bf16[8,4,64,768]{3,2,1,0:T(8,128)(2,1)S(1)} %copy.42) | copy-start | bytes 9437188
  175.8 30.3 %copy-start.61 = (bf16[1,8,96,1024]{3,2,1,0:T(8,128)(2,1)}, bf16[1,8,96,1024]{3,2,1,0:T(8,128)(2,1)S(1)}, u32[]{:S(2)}) copy-start(bf16[1,8,96,1024]{3,2,1,0:T(8,128)(2,1)S(1)} %get-tuple-element.55) | copy-start | bytes 4718596
  175.9 30.3 %copy-start.62 = (bf16[1,8,96,1024]{3,2,1,0:T(8,128)(2,1)}, bf16[1,8,96,1024]{3,2,1,0:T(8,128)(2,1)S(1)}, u32[]{:S(2)}) copy-start(bf16[1,8,96,1024]{3,2,1,0:T(8,128)(2,1)S(1)} %get-tuple-element.56) | copy-start | bytes 4718596
  175.9 31.6 %copy-start.57 = (bf16[1,8,96,1024]{3,2,1,0:T(8,128)(2,1)}, bf16[1,8,96,1024]{3,2,1,0:T(8,128)(2,1)S(1)}, u32[]{:S(2)}) copy-start(bf16[1,8,96,1024]{3,2,1,0:T(8,128)(2,1)S(1)} %get-tuple-element.54) | copy-start | bytes 4718596
  175.9 31.6 %copy-start.59 = (bf16[1,8,96,1024]{3,2,1,0:T(8,128)(2,1)}, bf16[1,8,96,1024]{3,2,1,0:T(8,128)(2,1)S(1)}, u32[]{:S(2)}) copy-start(bf16[1,8,96,1024]{3,2,1,0:T(8,128)(2,1)S(1)} %get-tuple-element.57) | copy-start | bytes 4718596
  175.9 2.2 copy-start.31
  176.4 20.5 %copy-start.5 = (bf16[256,768]{1,0:T(8,128)(2,1)}, bf16[256,768]{1,0:T(8,128)(2,1)S(1)}, u32[]{:S(2)}) copy-start(bf16[256,768]{1,0:T(8,128)(2,1)S(1)} %fusion.34.values_ref) | copy-start | bytes 1179652
  176.5 2.2 copy-start.41
  176.5 3.4 copy-start.44
  176.5 3.4 copy-start.75
  178.5 18.4 %copy-start.7 = (bf16[256,768]{1,0:T(8,128)(2,1)}, bf16[256,768]{1,0:T(8,128)(2,1)S(1)}, u32[]{:S(2)}) copy-start(bf16[256,768]{1,0:T(8,128)(2,1)S(1)} %fusion.33.keys_ref) | copy-start | bytes 1179652
  180.6 2.6 copy-start.13
  183.1 11.9 %copy-start.17 = (bf16[384,768]{1,0:T(8,128)(2,1)}, bf16[384,768]{1,0:T(8,128)(2,1)S(1)}, u32[]{:S(2)}) copy-start(bf16[384,768]{1,0:T(8,128)(2,1)S(1)} %convolution_convert_fusion.16.query_ref) | copy-start | bytes 1769476
  183.1 11.9 %copy-start.33 = (bf16[1,8,96,768]{3,2,1,0:T(8,128)(2,1)S(1)}, bf16[1,8,96,768]{3,2,1,0:T(8,128)(2,1)}, u32[]{:S(2)}) copy-start(bf16[1,8,96,768]{3,2,1,0:T(8,128)(2,1)} %get-tuple-element.47) | copy-start | bytes 3538948
  195.7 7.7 %copy-start.19 = (f32[384,768]{1,0:T(8,128)}, f32[384,768]{1,0:T(8,128)S(1)}, u32[]{:S(2)}) copy-start(f32[384,768]{1,0:T(8,128)S(1)} %get-tuple-element.70) | copy-start | bytes 3538948
  197.0 6.4 %copy-start.35 = (bf16[1,8,96,768]{3,2,1,0:T(8,128)(2,1)S(1)}, bf16[1,8,96,768]{3,2,1,0:T(8,128)(2,1)}, u32[]{:S(2)}) copy-start(bf16[1,8,96,768]{3,2,1,0:T(8,128)(2,1)} %get-tuple-element.43) | copy-start | bytes 3538948
  218.4 102.0 %reduce-scatter.5.cloned.1.call-start = ((), (), s32[]{:S(2)}) async-start(), calls=%async_computation.4 | async-start | bytes 5308416 | tf_op jit(solution)/shard_map/reduce_scatter | solution.py:381
  218.5 4.0 copy-start.38
  218.5 4.0 copy-start.58
  218.5 4.0 copy-start.60
  218.5 4.1 copy-start.88
  226.0 15.0 %copy-start.25 = (f32[384,768]{1,0:T(8,128)}, f32[384,768]{1,0:T(8,128)S(1)}, u32[]{:S(2)}) copy-start(f32[384,768]{1,0:T(8,128)S(1)} %fusion.41) | copy-start | bytes 3538948
  227.6 12.1 %copy-start.20 = (f32[384,768]{1,0:T(8,128)S(1)}, f32[384,768]{1,0:T(8,128)}, u32[]{:S(2)}) copy-start(f32[384,768]{1,0:T(8,128)} %copy-done.19) | copy-start | bytes 3538948
  227.6 12.1 %copy-start.28 = (bf16[1,8,96,768]{3,2,1,0:T(8,128)(2,1)S(1)}, bf16[1,8,96,768]{3,2,1,0:T(8,128)(2,1)}, u32[]{:S(2)}) copy-start(bf16[1,8,96,768]{3,2,1,0:T(8,128)(2,1)} %get-tuple-element.46) | copy-start | bytes 3538948
  242.3 21.5 %copy-start.23 = (f32[384,768]{1,0:T(8,128)}, f32[384,768]{1,0:T(8,128)S(1)}, u32[]{:S(2)}) copy-start(f32[384,768]{1,0:T(8,128)S(1)} %fusion.42) | copy-start | bytes 3538948
  244.2 16.8 %copy-start.42 = (bf16[1,384,768]{2,1,0:T(8,128)(2,1)S(1)}, bf16[1,384,768]{2,1,0:T(8,128)(2,1)}, u32[]{:S(2)}) copy-start(bf16[1,384,768]{2,1,0:T(8,128)(2,1)} %param.14) | copy-start | bytes 1769476
  244.2 16.8 %copy-start.76 = (f32[384]{0:T(512)S(1)}, f32[384]{0:T(512)}, u32[]{:S(2)}) copy-start(f32[384]{0:T(512)} %fusion.70) | copy-start | bytes 4612
  261.0 1.9 copy-start.3
  267.1 108.8 %reduce-scatter.7.cloned.1.call-start = ((), (), s32[]{:S(2)}) async-start(), calls=%async_computation.5 | async-start | bytes 5308416 | tf_op jit(solution)/shard_map/reduce_scatter | solution.py:381
  273.6 172.7 %reduce-scatter.9.cloned.1.call-start = ((), (), s32[]{:S(2)}) async-start(), calls=%async_computation.6 | async-start | bytes 7077888 | tf_op jit(solution)/shard_map/reduce_scatter | solution.py:381
  274.7 3.4 copy-start.87
  283.1 239.9 %all-reduce.4.cloned.1.call-start = ((), (), s32[]{:S(2)}) async-start(), calls=%async_computation.9 | async-start | bytes 4718592 | tf_op jit(solution)/shard_map/psum | solution.py:382
  446.3 3.7 copy-start.84
  446.4 3.7 copy-start.81
  446.4 3.8 copy-start.10
  446.4 44.0 %copy-start.78 = (f32[384]{0:T(512)S(1)}, f32[384]{0:T(512)}, u32[]{:S(2)}) copy-start(f32[384]{0:T(512)} %copy-done.77) | copy-start | bytes 4612
  446.4 44.0 %copy-start.32 = (bf16[1,8,96,768]{3,2,1,0:T(8,128)(2,1)S(1)}, bf16[1,8,96,768]{3,2,1,0:T(8,128)(2,1)}, u32[]{:S(2)}) copy-start(bf16[1,8,96,768]{3,2,1,0:T(8,128)(2,1)} %get-tuple-element.45) | copy-start | bytes 3538948
  491.8 2.3 copy-start.49
  491.8 3.6 copy-start.51
  (48 other events, 59.7 us)
Sparse Core Ops, SparseCore 0:
  12.0 131.0 all-gather.2
  218.5 38.4 reduce-scatter.10
  267.3 53.1 reduce-scatter.4
  322.6 53.3 reduce-scatter.6
  378.1 68.1 reduce-scatter.8
  449.5 73.3 all-reduce.3
